TPU v7x, 512 devices: a whole 4x8x8 slice. The times are simulated.
512 devices in a mesh: dp: 2 (over y_lo), head: 8 (over z), ctx: 32 (over y_hi, x, core).
Axes of the slice: x: 4, y: 8 (y_hi: 4, y_lo: 2; y = y_hi * 2 + y_lo), z: 8, core: 2. Of those that a mesh axis runs over, the one named last changes fastest.
Arguments:
- queries: bfloat16 [2, 8192, 5120], P('dp', 'ctx', 'head'), may hold values from -1.796875 to 1.796875
- keys: bfloat16 [2, 8192, 5120], P('dp', 'ctx', 'head'), may hold values from -1.796875 to 1.796875
- values: bfloat16 [2, 8192, 5120], P('dp', 'ctx', 'head'), may hold values from -6 to 6
- grad_out: bfloat16 [2, 8192, 5120], P('dp', 'ctx', 'head'), may hold values from -6 to 6
- gain: bfloat16 [5120], P('head'), may hold values from 0.5 to 1.5
- order_flag: int32 [32], P('ctx'), may hold values from 0 to 1
Outputs:
- grad_queries: bfloat16 [2, 8192, 5120], P('dp', 'ctx', 'head')
- grad_keys: bfloat16 [2, 8192, 5120], P('dp', 'ctx', 'head')
- grad_values: bfloat16 [2, 8192, 5120], P('dp', 'ctx', 'head')
- grad_gain: float32 [5120], P('head')
All inputs are finite; a program needn't handle non-finite values.
Results may differ from a plain program's by a relative error of at most 0.0014.
Values sent between devices are 32-bit elements; how exact they have to be, the bound alone decides.
A program may use at most 128 MiB of HBM per device.

v0:
```python
import jax
import jax.numpy as jnp
from jax import lax
from jax.sharding import PartitionSpec as P

DH = 128


def entering(part, axis, combine, identity):
    place = lax.axis_index(axis)
    gathered = jax.tree.map(lambda a: lax.all_gather(a, axis), part)
    state = jax.tree.map(lambda a, e: jnp.zeros_like(a) + jnp.asarray(e, a.dtype), part, identity)

    def one(step, state):
        return combine(
            state, jax.tree.map(lambda a: lax.dynamic_index_in_dim(a, step, 0, False), gathered)
        )

    return lax.fori_loop(0, place, one, state)


def contract(form, left, right):
    return jnp.einsum(
        form, left, right, precision=lax.Precision.HIGHEST, preferred_element_type=jnp.float32
    )


def add_states(earlier, later):
    return jax.tree.map(jnp.add, earlier, later)


def shards(queries, keys, values, grad_out, gain, order_flag):
    half_rows = queries.shape[1] // 2
    width = queries.shape[2]
    head_count = width // DH
    flag_bit = order_flag[0]

    def split(array):
        rows = array[0]
        first = rows[:half_rows]
        second = rows[half_rows:]
        early = jnp.where(flag_bit == 0, first, second)
        late = jnp.where(flag_bit == 0, second, first)
        return jnp.stack([early, late]).reshape(2, half_rows, head_count, DH).astype(jnp.float32)

    def merge_back(array):
        early = array[0].reshape(half_rows, width)
        late = array[1].reshape(half_rows, width)
        first = jnp.where(flag_bit == 0, early, late)
        second = jnp.where(flag_bit == 0, late, early)
        return jnp.concatenate([first, second], axis=0)[None].astype(jnp.bfloat16)

    query_f = split(queries)
    key_f = split(keys)
    value_f = split(values)
    grad_f = split(grad_out)
    zero_state = jnp.zeros((head_count, DH, DH), jnp.float32)
    kv_state = contract("cshd,cshe->chde", key_f, value_f)
    state_early = kv_state[0]
    state_late = kv_state[1]
    before_early, before_late = entering(
        (state_early, state_late), "ctx", add_states, (zero_state, zero_state)
    )
    state_whole = lax.psum(state_early + state_late, "ctx")
    prefix_late = state_whole - before_late - state_late
    prefix = jnp.stack([before_early, prefix_late])
    rows_idx = lax.broadcasted_iota(jnp.int32, (half_rows, half_rows), 0)
    cols_idx = lax.broadcasted_iota(jnp.int32, (half_rows, half_rows), 1)
    causal = (rows_idx >= cols_idx).astype(jnp.float32)
    scores = contract("cthd,cshd->chts", query_f, key_f) * causal
    attn = contract("chts,cshe->cthe", scores, value_f) + contract(
        "cthd,chde->cthe", query_f, prefix
    )
    gain_h = gain.astype(jnp.float32).reshape(1, 1, head_count, DH)
    upstream = grad_f * gain_h
    square_sum = jnp.sum(attn * attn, axis=(2, 3))
    cross_part = jnp.sum(upstream * attn, axis=(2, 3))
    square_all, cross_all = lax.psum((square_sum, cross_part), "head")
    features = width * lax.axis_size("head")
    inverse = lax.rsqrt(square_all / features + 1e-06)
    grad_attn = (
        upstream * inverse[:, :, None, None]
        - attn * (cross_all * inverse**3 / features)[:, :, None, None]
    )
    gain_part = jnp.sum(grad_f * attn * inverse[:, :, None, None], axis=(0, 1)).reshape(-1)
    grad_gain = lax.psum(gain_part, ("dp", "ctx"))
    adjoint = contract("cthd,cthe->chde", query_f, grad_attn)
    adjoint_early = adjoint[0]
    adjoint_late = adjoint[1]
    lower_early, lower_late = entering(
        (adjoint_early, adjoint_late), "ctx", add_states, (zero_state, zero_state)
    )
    adjoint_whole = lax.psum(adjoint_early + adjoint_late, "ctx")
    suffix_early = adjoint_whole - lower_early - adjoint_early
    suffix = jnp.stack([suffix_early, lower_late])
    grad_scores = contract("cthe,cshe->chts", grad_attn, value_f) * causal
    grad_q = contract("chts,cshd->cthd", grad_scores, key_f) + contract(
        "cthe,chde->cthd", grad_attn, prefix
    )
    grad_k = contract("chts,cthd->cshd", grad_scores, query_f) + contract(
        "cshe,chde->cshd", value_f, suffix
    )
    grad_v = contract("chts,cthe->cshe", scores, grad_attn) + contract(
        "cshd,chde->cshe", key_f, suffix
    )
    return (merge_back(grad_q), merge_back(grad_k), merge_back(grad_v), grad_gain)


def solution(mesh):
    in_specs = (
        P("dp", "ctx", "head"),
        P("dp", "ctx", "head"),
        P("dp", "ctx", "head"),
        P("dp", "ctx", "head"),
        P("head"),
        P("ctx"),
    )
    out_specs = (P("dp", "ctx", "head"), P("dp", "ctx", "head"), P("dp", "ctx", "head"), P("head"))
    return jax.shard_map(shards, mesh=mesh, in_specs=in_specs, out_specs=out_specs, check_vma=False)
```

profile of v0, /device:TPU:1, one launch (start us, length us, event | category | flops | bytes accessed | tf_op | source)
XLA Modules:
  0.0 994.3 jit_solution(7909327211450567344)
XLA Ops:
  7.2 1.1 fusion.34
  8.5 0.2 copy.109
  9.3 1.0 fusion.33
  10.5 0.2 copy.105
  10.9 0.2 copy.64
  11.1 0.4 fusion.22
  11.5 0.9 fusion.30
  12.5 0.7 all-gather.7.cloned.1.call-update
  13.2 0.8 bitcast_add_fusion.5
  14.1 1.0 fusion.32
  15.3 0.2 copy.111
  15.7 0.2 copy.72
  15.8 0.4 convolution_multiply_fusion.1
  16.2 1.7 fusion.23
  18.1 0.2 copy.107
  18.3 88.2 %all-gather.5.cloned.1.call-done = f32[32,5,128,128]{3,2,1,0:T(8,128)} async-done(((f32[1,5,128,128]{3,2,1,0:T(8,128)}), f32[32,5,128,128]{3,2,1,0:T(8,128)}) %all-gather.5.cloned.1.call-update) | async-done | bytes 10485776 | tf_op jit(solution)/shard_map/all_gather | solution.py:11
  106.5 95.3 %all-gather.7.cloned.1.call-done = f32[32,5,128,128]{3,2,1,0:T(8,128)} async-done(((f32[1,5,128,128]{3,2,1,0:T(8,128)}), f32[32,5,128,128]{3,2,1,0:T(8,128)}) %all-gather.7.cloned.1.call-update) | async-done | bytes 10485776 | tf_op jit(solution)/shard_map/all_gather | solution.py:11
  201.8 1.3 while.24
  201.8 1.2 bitcast_add_fusion.8
  203.1 277.9 %all-reduce.3.cloned.1.call-done = f32[5,128,128]{2,1,0:T(8,128)} async-done(((f32[5,128,128]{2,1,0:T(8,128)}), f32[5,128,128]{2,1,0:T(8,128)}) %all-reduce.3.cloned.1.call-update) | async-done | bytes 327696 | tf_op jit(solution)/shard_map/psum | solution.py:64
  481.0 1.0 fusion.12
  482.0 1.8 multiply_reduce_fusion
  483.8 14.3 %psum.36 = f32[2,128]{1,0:T(2,128)S(1)} all-reduce(f32[2,128]{1,0:T(2,128)S(1)} %get-tuple-element.132), channel_id=1, replica_groups=mesh['dp'=2,'head'=8,'ctx'=32] {'head'}, use_global_device_ids=true, to_apply=%region_4.5 | all-reduce | flops 256 | bytes 2048 | tf_op jit(solution)/shard_map/psum | solution.py:78
  498.2 0.3 fusion.9
  498.5 11.3 %psum.37 = f32[2,128]{1,0:T(2,128)S(1)} all-reduce(f32[2,128]{1,0:T(2,128)S(1)} %get-tuple-element.77), channel_id=1, replica_groups=mesh['dp'=2,'head'=8,'ctx'=32] {'head'}, use_global_device_ids=true, to_apply=%region_6.7 | all-reduce | flops 256 | bytes 2048 | tf_op jit(solution)/shard_map/psum | solution.py:78
  509.8 0.9 fusion.20
  510.8 0.9 fusion.29
  511.8 0.5 all-gather.11.cloned.1.call-update
  512.3 0.9 fusion.10
  513.2 1.8 convolution_multiply_fusion
  515.0 1.8 fusion.2
  516.9 0.7 select_convert_fusion.5
  517.6 1.7 copy.82
  519.3 1.7 copy.81
  521.1 140.1 %psum.39 = f32[640]{0:T(1024)} all-reduce(f32[640]{0:T(1024)S(1)} %bitcast.95), channel_id=1, replica_groups=mesh['dp'=2,'head'=8,'ctx'=32] {'dp','ctx'}, use_global_device_ids=true, to_apply=%region_11.12 | all-reduce | flops 640 | bytes 5120 | tf_op jit(solution)/shard_map/psum | solution.py:86
  661.2 1.7 pad_maximum_fusion.10
  662.9 0.8 bitcast_add_fusion.4
  663.7 2.3 fusion.21
  666.0 1.8 fusion.24
  667.8 35.8 %all-gather.11.cloned.1.call-done = f32[32,5,128,128]{3,2,1,0:T(8,128)} async-done(((f32[1,5,128,128]{3,2,1,0:T(8,128)}), f32[32,5,128,128]{3,2,1,0:T(8,128)}) %all-gather.11.cloned.1.call-update) | async-done | bytes 10485776 | tf_op jit(solution)/shard_map/all_gather | solution.py:11
  703.7 1.3 while.25
  703.7 1.2 bitcast_add_fusion.9
  705.0 277.0 %all-reduce.5.cloned.1.call-done = f32[5,128,128]{2,1,0:T(8,128)} async-done(((f32[5,128,128]{2,1,0:T(8,128)}), f32[5,128,128]{2,1,0:T(8,128)}) %all-reduce.5.cloned.1.call-update) | async-done | bytes 327696 | tf_op jit(solution)/shard_map/psum | solution.py:93
  981.9 1.0 fusion.11
  983.0 1.8 fusion
  984.8 0.4 fusion.1
  986.0 0.8 pad_maximum_fusion.11
  986.7 0.8 pad_maximum_fusion.12
  (59 shorter events, 2.3 us)
Async XLA Ops:
  7.2 10.7 %copy-start.10 = (bf16[1,256,640]{2,1,0:T(8,128)(2,1)S(1)}, bf16[1,256,640]{2,1,0:T(8,128)(2,1)}, u32[]{:S(2)}) copy-start(bf16[1,256,640]{2,1,0:T(8,128)(2,1)} %param.13) | copy-start | bytes 983044
  7.2 11.1 %copy-start.11 = (bf16[640]{0:T(1024)(128)(2,1)S(1)}, bf16[640]{0:T(1024)(128)(2,1)}, u32[]{:S(2)}) copy-start(bf16[640]{0:T(1024)(128)(2,1)} %param.14) | copy-start | bytes 3844
  7.2 99.3 %all-gather.5.cloned.1.call-start = ((), (), s32[]{:S(2)}) async-start(), calls=%async_computation | async-start | bytes 10813440 | tf_op jit(solution)/shard_map/all_gather | solution.py:11
  10.9 95.6 %copy-start.5 = (bf16[1,128,5,128]{3,1,2,0:T(8,128)(2,1)}, bf16[1,128,5,128]{3,1,2,0:T(8,128)(2,1)S(1)}, u32[]{:S(2)}) copy-start(bf16[1,128,5,128]{3,1,2,0:T(8,128)(2,1)S(1)} %copy.65) | copy-start | bytes 491524
  11.1 95.4 %copy-start.7 = (bf16[1,128,5,128]{3,1,2,0:T(8,128)(2,1)}, bf16[1,128,5,128]{3,1,2,0:T(8,128)(2,1)S(1)}, u32[]{:S(2)}) copy-start(bf16[1,128,5,128]{3,1,2,0:T(8,128)(2,1)S(1)} %copy.64) | copy-start | bytes 491524
  11.1 7.1 copy-start.1
  11.1 7.1 copy-start.3
  12.4 189.3 %all-gather.7.cloned.1.call-start = ((), (), s32[]{:S(2)}) async-start(), calls=%async_computation.1 | async-start | bytes 10813440 | tf_op jit(solution)/shard_map/all_gather | solution.py:11
  13.2 467.8 %all-reduce.3.cloned.1.call-start = ((), (), s32[]{:S(2)}) async-start(), calls=%async_computation.2 | async-start | bytes 655360 | tf_op jit(solution)/shard_map/psum | solution.py:64
  14.0 653.8 %all-gather.9.cloned.1.call-start = ((), (), s32[]{:S(2)}) async-start(), calls=%async_computation.4 | async-start | bytes 10813440 | tf_op jit(solution)/shard_map/all_gather | solution.py:11
  15.8 495.0 %copy-start = (bf16[1,128,5,128]{3,1,2,0:T(8,128)(2,1)}, bf16[1,128,5,128]{3,1,2,0:T(8,128)(2,1)S(1)}, u32[]{:S(2)}) copy-start(bf16[1,128,5,128]{3,1,2,0:T(8,128)(2,1)S(1)} %copy.72) | copy-start | bytes 491524
  511.7 191.9 %all-gather.11.cloned.1.call-start = ((), (), s32[]{:S(2)}) async-start(), calls=%async_computation.5 | async-start | bytes 10813440 | tf_op jit(solution)/shard_map/all_gather | solution.py:11
  512.3 469.7 %all-reduce.5.cloned.1.call-start = ((), (), s32[]{:S(2)}) async-start(), calls=%async_computation.3 | async-start | bytes 655360 | tf_op jit(solution)/shard_map/psum | solution.py:93
  516.9 467.9 %copy-start.2 = (bf16[1,128,640]{1,2,0:T(8,128)(2,1)S(1)}, bf16[1,128,640]{1,2,0:T(8,128)(2,1)}, u32[]{:S(2)}) copy-start(bf16[1,128,640]{1,2,0:T(8,128)(2,1)} %copy-done.1) | copy-start | bytes 491524
  516.9 467.9 %copy-start.4 = (bf16[1,128,640]{1,2,0:T(8,128)(2,1)S(1)}, bf16[1,128,640]{1,2,0:T(8,128)(2,1)}, u32[]{:S(2)}) copy-start(bf16[1,128,640]{1,2,0:T(8,128)(2,1)} %copy-done.3) | copy-start | bytes 491524
  666.0 317.0 %copy-start.6 = (bf16[1,128,5,128]{3,1,2,0:T(8,128)(2,1)S(1)}, bf16[1,128,5,128]{3,1,2,0:T(8,128)(2,1)}, u32[]{:S(2)}) copy-start(bf16[1,128,5,128]{3,1,2,0:T(8,128)(2,1)} %copy-done.5) | copy-start | bytes 491524
  666.0 317.0 %copy-start.8 = (bf16[1,128,5,128]{3,1,2,0:T(8,128)(2,1)S(1)}, bf16[1,128,5,128]{3,1,2,0:T(8,128)(2,1)}, u32[]{:S(2)}) copy-start(bf16[1,128,5,128]{3,1,2,0:T(8,128)(2,1)} %copy-done.7) | copy-start | bytes 491524
  667.8 317.0 %copy-start.9 = (f32[2,5,128,128]{3,2,1,0:T(8,128)S(1)}, f32[2,5,128,128]{3,2,1,0:T(8,128)}, u32[]{:S(2)}) copy-start(f32[2,5,128,128]{3,2,1,0:T(8,128)} %fusion.21) | copy-start | bytes 1966084
Sparse Core Ops, SparseCore 0:
  12.5 93.8 all-gather.4
  110.2 91.5 all-gather.6
  205.2 275.6 all-reduce.2
  511.8 95.0 all-gather.8
  610.9 92.6 all-gather.10
  706.7 275.2 all-reduce.4
where the time goes:
time: 997 us; the launch traced here: 994 us
  waiting for transfers between devices  775 us (78%)
  blocking collectives  166 us (17%)
  matrix products  15.9 us (2%)
  between operations  15.1 us (2%)
  local copies, waits for them, and re-layouts  11.2 us (1%)
  other arithmetic  10.6 us (1%)
    psum x1, waiting for transfers between devices, shards(): state_whole = lax.psum(state_early + state_late, 'ctx')  278 us
    psum x1, waiting for transfers between devices, shards(): adjoint_whole = lax.psum(adjoint_early + adjoint_late, 'ctx')  277 us
    all_gather x4, waiting for transfers between devices, entering(): gathered = jax.tree.map(lambda a: lax.all_gather(a, axis), part)  219 us
    psum x1, blocking collectives, shards(): grad_gain = lax.psum(gain_part, ('dp', 'ctx'))  140 us
    psum x2, blocking collectives, shards(): square_all, cross_all = lax.psum((square_sum, cross_part), 'head')  25.7 us
  transfers between devices with their start and end apart: 6, of which 5 were waited for; matrix products, arithmetic and copies ran while one was open for 2% of the time, Pallas kernels for 0%

commit v1 on v0

v1 whole, which is shorter than its diff:
```python
import jax
import jax.numpy as jnp
from jax import lax
from jax.experimental import pallas as pl
from jax.experimental.pallas import tpu as pltpu
from jax.sharding import PartitionSpec as P

MESH = pl.DeviceIdType.MESH
D = 128
NX, NY, NZ = 4, 4, 8
HEADS = 5
PART = D // NX
CHUNKS = ((0, 2), (2, 4), (4, 5))
NC = len(CHUNKS)
F32, BF16 = jnp.float32, jnp.bfloat16


def mm(a, b, ca, cb):
    return lax.dot_general(a, b, (((ca,), (cb,)), ((), ())), preferred_element_type=F32)


def parts(x):
    hi = x.astype(BF16)
    return hi, (x - hi.astype(F32)).astype(BF16)


def wide(*a):
    return jnp.concatenate(a, axis=1)


def tall(*a):
    return jnp.concatenate(a, axis=0)


def kernel(
    flag_ref, gain_ref, q_hbm, k_hbm, v_hbm, g_hbm,
    oq_hbm, ok_hbm, ov_hbm, gg_ref,
    q_ref, k_ref, v_ref, g_ref, oq_ref, ok_ref, ov_ref,
    x_st, y_st, r1, z_st, xr, w_st, yr, base, o_st, t_st, u_st, r2,
    attn, s_hi, s_lo, p_hi, p_lo, a_hi, a_lo, gk_loc, gv_loc,
    sq, cr, inv_b, coef_b, zbuf, gcore, gx, gy, gdp,
    in_sem, out_sem, c1_s, c1_r, x1_s, x1_r, y_s, y_r, x2_s, x2_r, c2_s, c2_r,
    z_s, z_r, gc_s, gc_r, gx_s, gx_r, gy_s, gy_r, gd_s, gd_r,
):
    dp = lax.axis_index("dp")
    z = lax.axis_index("head")
    ctx = lax.axis_index("ctx")
    core = lax.rem(ctx, 2)
    x = lax.rem(ctx // 2, NX)
    y = ctx // (2 * NX)
    sx = jnp.where(core == 0, x, NX - 1 - x)
    sy = jnp.where(core == 0, y, NY - 1 - y)

    def at(yy, xx, cc):
        return {"ctx": (yy * NX + xx) * 2 + cc}

    sibling = at(y, x, 1 - core)
    xs = [lax.rem(x + d, NX) for d in range(1, NX)]
    ys = [lax.rem(y + d, NY) for d in range(1, NY)]
    zs = [lax.rem(z + d, NZ) for d in range(1, NZ)]

    def remote(src, dst, ssem, rsem, device):
        return pltpu.make_async_remote_copy(
            src_ref=src, dst_ref=dst, send_sem=ssem, recv_sem=rsem, device_id=device, device_id_type=MESH
        )

    loads = []
    for i, (src, dst) in enumerate(((k_hbm, k_ref), (v_hbm, v_ref), (q_hbm, q_ref), (g_hbm, g_ref))):
        cp = pltpu.make_async_copy(src, dst, in_sem.at[i])
        cp.start()
        loads.append(cp)

    bar = pltpu.get_barrier_semaphore()
    peers = [sibling] + [at(y, v, core) for v in xs] + [at(v, x, core) for v in ys]
    peers += [{"head": v} for v in zs] + [{"dp": 1 - dp}]
    for p in peers:
        pl.semaphore_signal(bar, inc=1, device_id=p, device_id_type=MESH)

    flag = flag_ref[0]
    first0 = jnp.full((D, D), flag, jnp.int32) == 0
    low = jnp.full((D, D), core, jnp.int32) == 0
    causal = lax.broadcasted_iota(jnp.int32, (D, D), 0) >= lax.broadcasted_iota(jnp.int32, (D, D), 1)
    sends = []

    def cols(h):
        return pl.ds(h * D, D)

    def rows(s):
        return pl.ds(s * D, D)

    def heads(chunk, body):
        for h in range(*chunk):
            body(h)

    def put_state(n, h, s0, s1, mask):
        first = jnp.where(mask, s0, s1)
        both = s0 + s1
        x_st[n, h] = jnp.where(low, first, both)
        y_st[n, h] = jnp.where(low, both, first)

    def stage_core(n, c):
        hs = pl.ds(CHUNKS[c][0], CHUNKS[c][1] - CHUNKS[c][0])
        cp = remote(y_st.at[n, hs], r1.at[n, hs], c1_s.at[n, c], c1_r.at[n, c], sibling)
        cp.start()
        sends.append(cp)
        return cp

    def stage_x(n, c, before):
        hs = pl.ds(CHUNKS[c][0], CHUNKS[c][1] - CHUNKS[c][0])
        before.wait_recv()
        z_st[n, hs] = x_st[n, hs] + r1[n, hs]
        out = []
        for d, xx in enumerate(xs):
            there = pl.multiple_of(xx * PART, PART)
            cp = remote(
                z_st.at[n, hs, pl.ds(there, PART)], xr.at[n, sx, hs], x1_s.at[n, c, d], x1_r.at[n, c, d],
                at(y, xx, core),
            )
            cp.start()
            out.append(cp)
        xr[n, sx, hs] = z_st[n, hs, pl.ds(pl.multiple_of(x * PART, PART), PART)]
        sends.extend(out)
        return out

    def stage_y(n, c, before):
        hs = pl.ds(CHUNKS[c][0], CHUNKS[c][1] - CHUNKS[c][0])
        for cp in before:
            cp.wait_recv()
        w_st[n, hs] = (xr[n, 0, hs] + xr[n, 1, hs]) + (xr[n, 2, hs] + xr[n, 3, hs])
        out = []
        for e in range(1, NY):
            yy = jnp.where(core == 0, lax.rem(y + e, NY), lax.rem(y + NY - e, NY))
            cp = remote(w_st.at[n, hs], yr.at[n, e - 1, hs], y_s.at[n, c, e - 1], y_r.at[n, c, e - 1], at(yy, x, core))

            @pl.when(sy + e < NY)
            def _():
                cp.start()

            out.append(cp)
        return out

    def stage_back(n, c, before):
        hs = pl.ds(CHUNKS[c][0], CHUNKS[c][1] - CHUNKS[c][0])
        base[n, hs] = jnp.zeros_like(base[n, hs])
        for e, cp in enumerate(before, 1):

            @pl.when(sy >= e)
            def _():
                cp.wait_recv()
                base[n, hs] += yr[n, e - 1, hs]

        total = base[n, hs]
        for t in range(NX):
            o_st[n, t, hs] = total
            if t < NX - 1:
                total = total + xr[n, t, hs]
        out = []
        here = pl.ds(pl.multiple_of(x * PART, PART), PART)
        for d, xx in enumerate(xs):
            t = jnp.where(core == 0, xx, NX - 1 - xx)
            cp = remote(o_st.at[n, t, hs], t_st.at[n, hs, here], x2_s.at[n, c, d], x2_r.at[n, c, d], at(y, xx, core))
            cp.start()
            out.append(cp)
        t_st[n, hs, here] = o_st[n, sx, hs]
        sends.extend(out)
        return out

    def stage_swap(n, c, before):
        hs = pl.ds(CHUNKS[c][0], CHUNKS[c][1] - CHUNKS[c][0])
        for cp in before:
            cp.wait_recv()
        u_st[n, hs] = t_st[n, hs] + x_st[n, hs]
        cp = remote(u_st.at[n, hs], r2.at[n, hs], c2_s.at[n, c], c2_r.at[n, c], sibling)
        cp.start()
        sends.append(cp)
        return cp

    def get_states(n, h, mask):
        mine, other = t_st[n, h], r2[n, h]
        own_first = jnp.where(low, x_st[n, h], y_st[n, h])
        first = jnp.where(low, mine, other)
        second = (mine + other) + own_first
        return jnp.where(mask, first, second), jnp.where(mask, second, first)

    loads[0].wait()
    loads[1].wait()
    c1 = []
    for c, chunk in enumerate(CHUNKS):

        def body(h):
            kv = [mm(k_ref[rows(s), cols(h)], v_ref[rows(s), cols(h)], 0, 0) for s in range(2)]
            put_state(0, h, kv[0], kv[1], first0)

        heads(chunk, body)
        if c == 0:
            pl.semaphore_wait(bar, len(peers))
        c1.append(stage_core(0, c))

    def local_attn(h):
        for s in range(2):
            scores = jnp.where(causal, mm(q_ref[rows(s), cols(h)], k_ref[rows(s), cols(h)], 1, 1), 0.0)
            hi, lo = parts(scores)
            s_hi[s, h] = hi
            s_lo[s, h] = lo
            vv = v_ref[rows(s), cols(h)]
            attn[s, h] = mm(wide(hi, lo), tall(vv, vv), 1, 0)

    x1 = [stage_x(0, c, c1[c]) for c in range(NC)]
    loads[2].wait()
    loads[3].wait()
    heads((0, 2), local_attn)
    yy = [stage_y(0, c, x1[c]) for c in range(NC)]
    heads((2, 4), local_attn)
    x2 = [stage_back(0, c, yy[c]) for c in range(NC)]
    heads((4, 5), local_attn)
    c2 = [stage_swap(0, c, x2[c]) for c in range(NC)]

    gain = gain_ref[...].astype(F32)
    for c, chunk in enumerate(CHUNKS):
        c2[c].wait_recv()

        def body(h):
            prefix = get_states(0, h, first0)
            for s in range(2):
                hi, lo = parts(prefix[s])
                p_hi[s, h] = hi
                p_lo[s, h] = lo
                qq = q_ref[rows(s), cols(h)]
                a = attn[s, h] + mm(wide(qq, qq), tall(hi, lo), 1, 0)
                attn[s, h] = a
                up = g_ref[rows(s), cols(h)].astype(F32) * gain[:, h * D : (h + 1) * D]
                if h == 0:
                    sq[s] = a * a
                    cr[s] = up * a
                else:
                    sq[s] += a * a
                    cr[s] += up * a

        heads(chunk, body)

    zero = jnp.zeros((8 - 4, D), F32)
    zbuf[z] = tall(*[jnp.sum(jnp.transpose(m), axis=0, keepdims=True) for m in (sq[0], sq[1], cr[0], cr[1])], zero)
    zc = []
    for d, zz in enumerate(zs):
        cp = remote(zbuf.at[z], zbuf.at[z], z_s.at[d], z_r.at[d], {"head": zz})
        cp.start()
        zc.append(cp)
    sends.extend(zc)
    for cp in zc:
        cp.wait_recv()
    sums = zbuf[0]
    for i in range(1, NZ):
        sums = sums + zbuf[i]
    features = float(HEADS * D * NZ)
    inverse = lax.rsqrt(sums[0:2] * (1.0 / features) + 1e-6)
    coef = sums[2:4] * (inverse * inverse * inverse) * (1.0 / features)
    for s in range(2):
        inv_b[s] = jnp.transpose(jnp.broadcast_to(inverse[s : s + 1], (D, D)))
        coef_b[s] = jnp.transpose(jnp.broadcast_to(coef[s : s + 1], (D, D)))

    last0 = jnp.logical_not(first0)
    c1 = []
    for c, chunk in enumerate(CHUNKS):

        def body(h):
            adj = []
            for s in range(2):
                up = g_ref[rows(s), cols(h)].astype(F32) * gain[:, h * D : (h + 1) * D]
                hi, lo = parts(up * inv_b[s] - attn[s, h] * coef_b[s])
                a_hi[s, h] = hi
                a_lo[s, h] = lo
                qq = q_ref[rows(s), cols(h)]
                adj.append(mm(tall(qq, qq), tall(hi, lo), 0, 0))
            put_state(1, h, adj[0], adj[1], last0)

        heads(chunk, body)
        c1.append(stage_core(1, c))

    def local_grads(h):
        for s in range(2):
            ah, al = a_hi[s, h], a_lo[s, h]
            sh, sl = s_hi[s, h], s_lo[s, h]
            ph, pw = p_hi[s, h], p_lo[s, h]
            qq, kk, vv = (r[rows(s), cols(h)] for r in (q_ref, k_ref, v_ref))
            gs = jnp.where(causal, mm(wide(ah, al), wide(vv, vv), 1, 1), 0.0)
            gh, gl = parts(gs)
            gq = mm(wide(gh, gl), tall(kk, kk), 1, 0) + mm(wide(ah, al, ah), wide(ph, ph, pw), 1, 1)
            oq_ref[rows(s), cols(h)] = gq.astype(BF16)
            gk_loc[s, h] = mm(tall(gh, gl), tall(qq, qq), 0, 0)
            gv_loc[s, h] = mm(tall(sh, sl, sh), tall(ah, ah, al), 0, 0)

    def gain_terms():
        out = []
        for h in range(HEADS):
            terms = [g_ref[rows(s), cols(h)].astype(F32) * attn[s, h] * inv_b[s] for s in range(2)]
            out.append(jnp.sum(terms[0] + terms[1], axis=0, keepdims=True))
        return tall(*out, jnp.zeros((8 - HEADS, D), F32))

    def gain_send(buf, me, ssem, rsem, devices):
        out = []
        for d, device in enumerate(devices):
            cp = remote(buf.at[me], buf.at[me], ssem.at[d], rsem.at[d], device)
            cp.start()
            out.append(cp)
        sends.extend(out)
        return out

    def gain_sum(buf, count, copies):
        for cp in copies:
            cp.wait_recv()
        total = buf[0]
        for i in range(1, count):
            total = total + buf[i]
        return total

    x1 = [stage_x(1, c, c1[c]) for c in range(NC)]
    gcore[core] = gain_terms()
    gc = gain_send(gcore, core, gc_s, gc_r, [sibling])
    heads((0, 2), local_grads)
    yy = [stage_y(1, c, x1[c]) for c in range(NC)]
    gx[x] = gain_sum(gcore, 2, gc)
    gc = gain_send(gx, x, gx_s, gx_r, [at(y, v, core) for v in xs])
    heads((2, 4), local_grads)
    x2 = [stage_back(1, c, yy[c]) for c in range(NC)]
    gy[y] = gain_sum(gx, NX, gc)
    gc = gain_send(gy, y, gy_s, gy_r, [at(v, x, core) for v in ys])
    heads((4, 5), local_grads)
    store_q = pltpu.make_async_copy(oq_ref, oq_hbm, out_sem.at[0])
    store_q.start()
    c2 = [stage_swap(1, c, x2[c]) for c in range(NC)]
    gdp[dp] = gain_sum(gy, NY, gc)
    gc = gain_send(gdp, dp, gd_s, gd_r, [{"dp": 1 - dp}])

    for c, chunk in enumerate(CHUNKS):
        c2[c].wait_recv()

        def body(h):
            suffix = get_states(1, h, last0)
            for s in range(2):
                hi, lo = parts(suffix[s])
                kk, vv = (r[rows(s), cols(h)] for r in (k_ref, v_ref))
                gk = gk_loc[s, h] + mm(wide(vv, vv), wide(hi, lo), 1, 1)
                gv = gv_loc[s, h] + mm(wide(kk, kk), tall(hi, lo), 1, 0)
                ok_ref[rows(s), cols(h)] = gk.astype(BF16)
                ov_ref[rows(s), cols(h)] = gv.astype(BF16)

        heads(chunk, body)
    store_k = pltpu.make_async_copy(ok_ref, ok_hbm, out_sem.at[1])
    store_v = pltpu.make_async_copy(ov_ref, ov_hbm, out_sem.at[2])
    store_k.start()
    store_v.start()
    gg_ref[...] = gain_sum(gdp, 2, gc)

    for cp in sends:
        cp.wait_send()
    for n in range(2):
        for c, chunk in enumerate(CHUNKS):
            hs = pl.ds(chunk[0], chunk[1] - chunk[0])
            for e in range(1, NY):

                @pl.when(sy + e < NY)
                def _():
                    remote(
                        w_st.at[n, hs], yr.at[n, e - 1, hs], y_s.at[n, c, e - 1], y_r.at[n, c, e - 1], sibling
                    ).wait_send()

    store_q.wait()
    store_k.wait()
    store_v.wait()


def shards(queries, keys, values, grad_out, gain, order_flag):
    shape = queries.shape
    tokens, width = shape[1], shape[2]
    flat = [a.reshape(tokens, width) for a in (queries, keys, values, grad_out)]
    state = (2, HEADS, D, D)
    piece = (HEADS, PART, D)
    dma = pltpu.SemaphoreType.DMA
    scratch = [pltpu.VMEM((tokens, width), BF16)] * 7
    scratch += [pltpu.VMEM(state, F32)] * 4
    scratch += [
        pltpu.VMEM((2, NX) + piece, F32),
        pltpu.VMEM((2,) + piece, F32),
        pltpu.VMEM((2, NY - 1) + piece, F32),
        pltpu.VMEM((2,) + piece, F32),
        pltpu.VMEM((2, NX) + piece, F32),
    ]
    scratch += [pltpu.VMEM(state, F32)] * 3
    scratch += [pltpu.VMEM(state, F32)]
    scratch += [pltpu.VMEM(state, BF16)] * 6
    scratch += [pltpu.VMEM(state, F32)] * 2
    scratch += [pltpu.VMEM((2, D, D), F32)] * 4
    scratch += [pltpu.VMEM((n, 8, D), F32) for n in (NZ, 2, NX, NY, 2)]
    scratch += [dma((4,)), dma((3,))]
    for shape_of in ((2, NC), (2, NC, NX - 1), (2, NC, NY - 1), (2, NC, NX - 1), (2, NC)):
        scratch += [dma(shape_of)] * 2
    for count in (NZ - 1, 1, NX - 1, NY - 1, 1):
        scratch += [dma((count,))] * 2
    hbm = pl.BlockSpec(memory_space=pl.ANY)
    vmem = pl.BlockSpec(memory_space=pltpu.VMEM)
    out = jax.ShapeDtypeStruct((tokens, width), BF16)
    gq, gk, gv, gg = pl.pallas_call(
        kernel,
        name="layer_backward",
        out_shape=(out, out, out, jax.ShapeDtypeStruct((8, D), F32)),
        in_specs=[pl.BlockSpec(memory_space=pltpu.SMEM), vmem, hbm, hbm, hbm, hbm],
        out_specs=(hbm, hbm, hbm, vmem),
        scratch_shapes=scratch,
        compiler_params=pltpu.CompilerParams(
            collective_id=0, has_side_effects=True, vmem_limit_bytes=48 * 1024 * 1024
        ),
    )(order_flag, gain.reshape(1, width), *flat)
    return gq.reshape(shape), gk.reshape(shape), gv.reshape(shape), gg[:HEADS].reshape(width)


def solution(mesh):
    rows = P("dp", "ctx", "head")
    return jax.shard_map(
        shards,
        mesh=mesh,
        in_specs=(rows, rows, rows, rows, P("head"), P("ctx")),
        out_specs=(rows, rows, rows, P("head")),
        check_vma=False,
    )
```

time: 997 us -> 66.5 us (0.07)
  the two profiles are of different devices: /device:TPU:1 before, /device:TPU:16 now
where the time goes in v1:
time: 66.5 us; the launch traced here: 66.2 us
  Pallas kernels  57.6 us (87%)
  local copies, waits for them, and re-layouts  7.33 us (11%)
  between operations  1.3 us (2%)
    pallas_call x1, Pallas kernels, shards(): pl.pallas_call(kernel, name='layer_backward', out_shape=(out, out, out, j...  57.6 us
    unnamed x13, local copies, waits for them, and re-layouts  6.73 us

profile of v1, /device:TPU:16, one launch (start us, length us, event | category | flops | bytes accessed | tf_op | source)
XLA Modules:
  0.0 66.2 jit_solution(16718914352673090620)
XLA Ops:
  1.3 0.0 copy-start.4
  1.3 0.7 %copy-done.4 = bf16[640]{0:T(1024)(128)(2,1)S(1)} copy-done((bf16[640]{0:T(1024)(128)(2,1)S(1)}, bf16[640]{0:T(1024)(128)(2,1)}, u32[]{:S(2)}) %copy-start.4) | copy-done | bytes 1304
  2.0 0.0 copy-start
  2.0 1.0 %copy-done = bf16[1,256,640]{2,1,0:T(8,128)(2,1)S(1)} copy-done((bf16[1,256,640]{2,1,0:T(8,128)(2,1)S(1)}, bf16[1,256,640]{2,1,0:T(8,128)(2,1)}, u32[]{:S(2)}) %copy-start) | copy-done | bytes 327704
  2.9 0.0 copy-start.1
  2.9 1.0 %copy-done.1 = bf16[1,256,640]{2,1,0:T(8,128)(2,1)S(1)} copy-done((bf16[1,256,640]{2,1,0:T(8,128)(2,1)S(1)}, bf16[1,256,640]{2,1,0:T(8,128)(2,1)}, u32[]{:S(2)}) %copy-start.1) | copy-done | bytes 327704
  3.9 0.0 copy-start.2
  3.9 1.0 %copy-done.2 = bf16[1,256,640]{2,1,0:T(8,128)(2,1)S(1)} copy-done((bf16[1,256,640]{2,1,0:T(8,128)(2,1)S(1)}, bf16[1,256,640]{2,1,0:T(8,128)(2,1)}, u32[]{:S(2)}) %copy-start.2) | copy-done | bytes 327704
  4.9 0.0 copy-start.3
  4.9 1.0 %copy-done.3 = bf16[1,256,640]{2,1,0:T(8,128)(2,1)S(1)} copy-done((bf16[1,256,640]{2,1,0:T(8,128)(2,1)S(1)}, bf16[1,256,640]{2,1,0:T(8,128)(2,1)}, u32[]{:S(2)}) %copy-start.3) | copy-done | bytes 327704
  5.9 57.6 %layer_backward.1 = (bf16[256,640]{1,0:T(8,128)(2,1)S(1)}, bf16[256,640]{1,0:T(8,128)(2,1)S(1)}, bf16[256,640]{1,0:T(8,128)(2,1)S(1)}, f32[8,128]{1,0:T(8,128)S(1)}) custom-call(s32[1]{0:T(128)S(6)} %copy.13.flag_ref, bf16[1,640]{1,0:T(2,128)(2,1)S(1)} %reshape.35.gain_ref, bf16[256,640]{1,0:T(8,128)(2,1)S(1)} %bitcast.12, bf16[256,640]{1,0:T(8,128)(2,1)S(1)} %bitcast.13, ...), custom_call_target="tpu_custom_call" | custom-call | tf_op jit(solution)/shard_map/layer_backward/pallas_call | solution.py:402
  63.5 0.6 slice_bitcast_fusion
  64.1 0.7 %copy.14 = bf16[1,256,640]{2,1,0:T(8,128)(2,1)} copy(bf16[1,256,640]{2,1,0:T(8,128)(2,1)S(1)} %bitcast.11) | data formatting | bytes 655360
  64.8 0.7 %copy.15 = bf16[1,256,640]{2,1,0:T(8,128)(2,1)} copy(bf16[1,256,640]{2,1,0:T(8,128)(2,1)S(1)} %bitcast.10) | data formatting | bytes 655360
  65.5 0.7 %copy.16 = bf16[1,256,640]{2,1,0:T(8,128)(2,1)} copy(bf16[1,256,640]{2,1,0:T(8,128)(2,1)S(1)} %bitcast.9) | data formatting | bytes 655360
  (1 shorter events, 0.0 us)
Async XLA Ops:
  1.3 0.7 %copy-start.4 = (bf16[640]{0:T(1024)(128)(2,1)S(1)}, bf16[640]{0:T(1024)(128)(2,1)}, u32[]{:S(2)}) copy-start(bf16[640]{0:T(1024)(128)(2,1)} %param.10) | copy-start | bytes 3844
  2.0 1.0 %copy-start = (bf16[1,256,640]{2,1,0:T(8,128)(2,1)S(1)}, bf16[1,256,640]{2,1,0:T(8,128)(2,1)}, u32[]{:S(2)}) copy-start(bf16[1,256,640]{2,1,0:T(8,128)(2,1)} %param.6) | copy-start | bytes 983044
  2.9 1.0 %copy-start.1 = (bf16[1,256,640]{2,1,0:T(8,128)(2,1)S(1)}, bf16[1,256,640]{2,1,0:T(8,128)(2,1)}, u32[]{:S(2)}) copy-start(bf16[1,256,640]{2,1,0:T(8,128)(2,1)} %param.7) | copy-start | bytes 983044
  3.9 1.0 %copy-start.2 = (bf16[1,256,640]{2,1,0:T(8,128)(2,1)S(1)}, bf16[1,256,640]{2,1,0:T(8,128)(2,1)}, u32[]{:S(2)}) copy-start(bf16[1,256,640]{2,1,0:T(8,128)(2,1)} %param.8) | copy-start | bytes 983044
  4.9 1.0 %copy-start.3 = (bf16[1,256,640]{2,1,0:T(8,128)(2,1)S(1)}, bf16[1,256,640]{2,1,0:T(8,128)(2,1)}, u32[]{:S(2)}) copy-start(bf16[1,256,640]{2,1,0:T(8,128)(2,1)} %param.9) | copy-start | bytes 983044

commit v2 on v1

--- a/solution.py
+++ b/solution.py
@@ -10,8 +10,9 @@
 NX, NY, NZ = 4, 4, 8
 HEADS = 5
 PART = D // NX
-CHUNKS = ((0, 2), (2, 4), (4, 5))
+CHUNKS = tuple((h, h + 1) for h in range(HEADS))
 NC = len(CHUNKS)
+PIECES = 1
 F32, BF16 = jnp.float32, jnp.bfloat16
 
 
@@ -33,13 +34,13 @@
 
 
 def kernel(
-    flag_ref, gain_ref, q_hbm, k_hbm, v_hbm, g_hbm,
-    oq_hbm, ok_hbm, ov_hbm, gg_ref,
-    q_ref, k_ref, v_ref, g_ref, oq_ref, ok_ref, ov_ref,
+    flag_ref, gain_hbm, q_hbm, k_hbm, v_hbm, g_hbm,
+    oq_ref, ok_ref, ov_ref, gg_ref,
+    q_ref, k_ref, v_ref, g_ref, gain_ref,
     x_st, y_st, r1, z_st, xr, w_st, yr, base, o_st, t_st, u_st, r2,
-    attn, s_hi, s_lo, p_hi, p_lo, a_hi, a_lo, gk_loc, gv_loc,
+    attn, s_hi, s_lo, p_hi, p_lo, a_hi, a_lo, qt, up, gk_loc, gv_loc,
     sq, cr, inv_b, coef_b, zbuf, gcore, gx, gy, gdp,
-    in_sem, out_sem, c1_s, c1_r, x1_s, x1_r, y_s, y_r, x2_s, x2_r, c2_s, c2_r,
+    in_sem, kv_sem, c1_s, c1_r, x1_s, x1_r, y_s, y_r, x2_s, x2_r, c2_s, c2_r,
     z_s, z_r, gc_s, gc_r, gx_s, gx_r, gy_s, gy_r, gd_s, gd_r,
 ):
     dp = lax.axis_index("dp")
@@ -55,7 +56,7 @@
         return {"ctx": (yy * NX + xx) * 2 + cc}
 
     sibling = at(y, x, 1 - core)
-    xs = [lax.rem(x + d, NX) for d in range(1, NX)]
+    xs = [lax.rem(x + d, NX) for d in (2, 1, 3)]
     ys = [lax.rem(y + d, NY) for d in range(1, NY)]
     zs = [lax.rem(z + d, NZ) for d in range(1, NZ)]
 
@@ -64,17 +65,23 @@
             src_ref=src, dst_ref=dst, send_sem=ssem, recv_sem=rsem, device_id=device, device_id_type=MESH
         )
 
-    loads = []
-    for i, (src, dst) in enumerate(((k_hbm, k_ref), (v_hbm, v_ref), (q_hbm, q_ref), (g_hbm, g_ref))):
-        cp = pltpu.make_async_copy(src, dst, in_sem.at[i])
+    def load(src, dst, sem):
+        cp = pltpu.make_async_copy(src, dst, sem)
         cp.start()
-        loads.append(cp)
-
+        return cp
+
+    def load_head(h):
+        where = (slice(None), pl.ds(h * D, D))
+        return [load(src.at[where], dst.at[where], kv_sem.at[i, h]) for i, (src, dst) in enumerate(((k_hbm, k_ref), (v_hbm, v_ref)))]
+
+    kv_loads = [load_head(0)]
     bar = pltpu.get_barrier_semaphore()
     peers = [sibling] + [at(y, v, core) for v in xs] + [at(v, x, core) for v in ys]
     peers += [{"head": v} for v in zs] + [{"dp": 1 - dp}]
     for p in peers:
         pl.semaphore_signal(bar, inc=1, device_id=p, device_id_type=MESH)
+    kv_loads += [load_head(h) for h in range(1, HEADS)]
+    loads = [load(*c, in_sem.at[i]) for i, c in enumerate(((q_hbm, q_ref), (g_hbm, g_ref), (gain_hbm, gain_ref)))]
 
     flag = flag_ref[0]
     first0 = jnp.full((D, D), flag, jnp.int32) == 0
@@ -128,7 +135,7 @@
             cp.wait_recv()
         w_st[n, hs] = (xr[n, 0, hs] + xr[n, 1, hs]) + (xr[n, 2, hs] + xr[n, 3, hs])
         out = []
-        for e in range(1, NY):
+        for e in (2, 1, 3):
             yy = jnp.where(core == 0, lax.rem(y + e, NY), lax.rem(y + NY - e, NY))
             cp = remote(w_st.at[n, hs], yr.at[n, e - 1, hs], y_s.at[n, c, e - 1], y_r.at[n, c, e - 1], at(yy, x, core))
 
@@ -137,7 +144,7 @@
                 cp.start()
 
             out.append(cp)
-        return out
+        return [out[1], out[0], out[2]]
 
     def stage_back(n, c, before):
         hs = pl.ds(CHUNKS[c][0], CHUNKS[c][1] - CHUNKS[c][0])
@@ -182,12 +189,12 @@
         second = (mine + other) + own_first
         return jnp.where(mask, first, second), jnp.where(mask, second, first)
 
-    loads[0].wait()
-    loads[1].wait()
     c1 = []
     for c, chunk in enumerate(CHUNKS):
 
         def body(h):
+            for cp in kv_loads[h]:
+                cp.wait()
             kv = [mm(k_ref[rows(s), cols(h)], v_ref[rows(s), cols(h)], 0, 0) for s in range(2)]
             put_state(0, h, kv[0], kv[1], first0)
 
@@ -198,6 +205,8 @@
 
     def local_attn(h):
         for s in range(2):
+            qt[s, h] = jnp.transpose(q_ref[rows(s), cols(h)])
+            up[s, h] = g_ref[rows(s), cols(h)].astype(F32) * gain[:, h * D : (h + 1) * D]
             scores = jnp.where(causal, mm(q_ref[rows(s), cols(h)], k_ref[rows(s), cols(h)], 1, 1), 0.0)
             hi, lo = parts(scores)
             s_hi[s, h] = hi
@@ -206,16 +215,15 @@
             attn[s, h] = mm(wide(hi, lo), tall(vv, vv), 1, 0)
 
     x1 = [stage_x(0, c, c1[c]) for c in range(NC)]
-    loads[2].wait()
-    loads[3].wait()
+    for cp in loads:
+        cp.wait()
+    gain = gain_ref[...].astype(F32).reshape(1, HEADS * D)
     heads((0, 2), local_attn)
     yy = [stage_y(0, c, x1[c]) for c in range(NC)]
-    heads((2, 4), local_attn)
+    heads((2, 5), local_attn)
     x2 = [stage_back(0, c, yy[c]) for c in range(NC)]
-    heads((4, 5), local_attn)
     c2 = [stage_swap(0, c, x2[c]) for c in range(NC)]
 
-    gain = gain_ref[...].astype(F32)
     for c, chunk in enumerate(CHUNKS):
         c2[c].wait_recv()
 
@@ -228,13 +236,12 @@
                 qq = q_ref[rows(s), cols(h)]
                 a = attn[s, h] + mm(wide(qq, qq), tall(hi, lo), 1, 0)
                 attn[s, h] = a
-                up = g_ref[rows(s), cols(h)].astype(F32) * gain[:, h * D : (h + 1) * D]
                 if h == 0:
                     sq[s] = a * a
-                    cr[s] = up * a
+                    cr[s] = up[s, h] * a
                 else:
                     sq[s] += a * a
-                    cr[s] += up * a
+                    cr[s] += up[s, h] * a
 
         heads(chunk, body)
 
@@ -265,12 +272,11 @@
         def body(h):
             adj = []
             for s in range(2):
-                up = g_ref[rows(s), cols(h)].astype(F32) * gain[:, h * D : (h + 1) * D]
-                hi, lo = parts(up * inv_b[s] - attn[s, h] * coef_b[s])
+                hi, lo = parts(up[s, h] * inv_b[s] - attn[s, h] * coef_b[s])
                 a_hi[s, h] = hi
                 a_lo[s, h] = lo
-                qq = q_ref[rows(s), cols(h)]
-                adj.append(mm(tall(qq, qq), tall(hi, lo), 0, 0))
+                qq = qt[s, h]
+                adj.append(mm(wide(qq, qq), tall(hi, lo), 1, 0))
             put_state(1, h, adj[0], adj[1], last0)
 
         heads(chunk, body)
@@ -325,8 +331,6 @@
     gy[y] = gain_sum(gx, NX, gc)
     gc = gain_send(gy, y, gy_s, gy_r, [at(v, x, core) for v in ys])
     heads((4, 5), local_grads)
-    store_q = pltpu.make_async_copy(oq_ref, oq_hbm, out_sem.at[0])
-    store_q.start()
     c2 = [stage_swap(1, c, x2[c]) for c in range(NC)]
     gdp[dp] = gain_sum(gy, NY, gc)
     gc = gain_send(gdp, dp, gd_s, gd_r, [{"dp": 1 - dp}])
@@ -345,10 +349,6 @@
                 ov_ref[rows(s), cols(h)] = gv.astype(BF16)
 
         heads(chunk, body)
-    store_k = pltpu.make_async_copy(ok_ref, ok_hbm, out_sem.at[1])
-    store_v = pltpu.make_async_copy(ov_ref, ov_hbm, out_sem.at[2])
-    store_k.start()
-    store_v.start()
     gg_ref[...] = gain_sum(gdp, 2, gc)
 
     for cp in sends:
@@ -364,19 +364,29 @@
                         w_st.at[n, hs], yr.at[n, e - 1, hs], y_s.at[n, c, e - 1], y_r.at[n, c, e - 1], sibling
                     ).wait_send()
 
-    store_q.wait()
-    store_k.wait()
-    store_v.wait()
+
+def write_kernel(gq, gk, gv, gg, oq, ok, ov, og, sem):
+    copies = []
+    for i, (src, dst) in enumerate(((gq, oq), (gk, ok), (gv, ov))):
+        for j in range(PIECES):
+            rows = pl.ds(j * (src.shape[0] // PIECES), src.shape[0] // PIECES)
+            copies.append(pltpu.make_async_copy(src.at[rows], dst.at[rows], sem.at[i, j]))
+            copies[-1].start()
+    for h in range(HEADS):
+        og[pl.ds(h * D, D)] = gg[h]
+    for cp in copies:
+        cp.wait()
 
 
 def shards(queries, keys, values, grad_out, gain, order_flag):
     shape = queries.shape
     tokens, width = shape[1], shape[2]
     flat = [a.reshape(tokens, width) for a in (queries, keys, values, grad_out)]
+    gain = pltpu.with_memory_space_constraint(gain, pltpu.HBM)
     state = (2, HEADS, D, D)
     piece = (HEADS, PART, D)
     dma = pltpu.SemaphoreType.DMA
-    scratch = [pltpu.VMEM((tokens, width), BF16)] * 7
+    scratch = [pltpu.VMEM((tokens, width), BF16)] * 4 + [pltpu.VMEM((width,), BF16)]
     scratch += [pltpu.VMEM(state, F32)] * 4
     scratch += [
         pltpu.VMEM((2, NX) + piece, F32),
@@ -387,11 +397,11 @@
     ]
     scratch += [pltpu.VMEM(state, F32)] * 3
     scratch += [pltpu.VMEM(state, F32)]
-    scratch += [pltpu.VMEM(state, BF16)] * 6
-    scratch += [pltpu.VMEM(state, F32)] * 2
+    scratch += [pltpu.VMEM(state, BF16)] * 7
+    scratch += [pltpu.VMEM(state, F32)] * 3
     scratch += [pltpu.VMEM((2, D, D), F32)] * 4
     scratch += [pltpu.VMEM((n, 8, D), F32) for n in (NZ, 2, NX, NY, 2)]
-    scratch += [dma((4,)), dma((3,))]
+    scratch += [dma((3,)), dma((2, HEADS))]
     for shape_of in ((2, NC), (2, NC, NX - 1), (2, NC, NY - 1), (2, NC, NX - 1), (2, NC)):
         scratch += [dma(shape_of)] * 2
     for count in (NZ - 1, 1, NX - 1, NY - 1, 1):
@@ -399,18 +409,30 @@
     hbm = pl.BlockSpec(memory_space=pl.ANY)
     vmem = pl.BlockSpec(memory_space=pltpu.VMEM)
     out = jax.ShapeDtypeStruct((tokens, width), BF16)
+    inner = pltpu.VMEM((tokens, width), BF16)
+    flat = [pltpu.with_memory_space_constraint(a, pltpu.HBM) for a in flat]
     gq, gk, gv, gg = pl.pallas_call(
         kernel,
         name="layer_backward",
-        out_shape=(out, out, out, jax.ShapeDtypeStruct((8, D), F32)),
-        in_specs=[pl.BlockSpec(memory_space=pltpu.SMEM), vmem, hbm, hbm, hbm, hbm],
-        out_specs=(hbm, hbm, hbm, vmem),
+        out_shape=(inner, inner, inner, jax.ShapeDtypeStruct((8, D), F32)),
+        in_specs=[pl.BlockSpec(memory_space=pltpu.SMEM), hbm, hbm, hbm, hbm, hbm],
+        out_specs=(vmem, vmem, vmem, vmem),
         scratch_shapes=scratch,
         compiler_params=pltpu.CompilerParams(
-            collective_id=0, has_side_effects=True, vmem_limit_bytes=48 * 1024 * 1024
+            collective_id=0, has_side_effects=True, vmem_limit_bytes=32 * 1024 * 1024
         ),
-    )(order_flag, gain.reshape(1, width), *flat)
-    return gq.reshape(shape), gk.reshape(shape), gv.reshape(shape), gg[:HEADS].reshape(width)
+    )(order_flag, gain, *flat)
+    gq, gk, gv = [pltpu.with_memory_space_constraint(a, pltpu.VMEM) for a in (gq, gk, gv)]
+    gq, gk, gv, gg = pl.pallas_call(
+        write_kernel,
+        name="write_results",
+        out_shape=(out, out, out, jax.ShapeDtypeStruct((width,), F32)),
+        in_specs=[vmem, vmem, vmem, vmem],
+        out_specs=(hbm, hbm, hbm, vmem),
+        scratch_shapes=[dma((3, PIECES))],
+        compiler_params=pltpu.CompilerParams(vmem_limit_bytes=32 * 1024 * 1024),
+    )(gq, gk, gv, gg)
+    return gq.reshape(shape), gk.reshape(shape), gv.reshape(shape), gg
 
 
 def solution(mesh):

time: 66.5 us -> 59 us (0.89)
  the two profiles are of different devices: /device:TPU:16 before, /device:TPU:8 now
where the time goes in v2:
time: 59 us; the launch traced here: 58.9 us
  Pallas kernels  57.6 us (98%)
  between operations  1.29 us (2%)
    pallas_call x1, Pallas kernels, shards(): pl.pallas_call(kernel, name='layer_backward', out_shape=(inner, inner, in...  56.1 us
    pallas_call x1, Pallas kernels, shards(): pl.pallas_call(write_kernel, name='write_results', out_shape=(out, out, o...  1.55 us

profile of v2, /device:TPU:8, one launch (start us, length us, event | category | flops | bytes accessed | tf_op | source)
XLA Modules:
  0.0 58.9 jit_solution(10066051595925101056)
XLA Ops:
  1.3 56.1 %layer_backward.1 = (bf16[256,640]{1,0:T(8,128)(2,1)S(1)}, bf16[256,640]{1,0:T(8,128)(2,1)S(1)}, bf16[256,640]{1,0:T(8,128)(2,1)S(1)}, f32[8,128]{1,0:T(8,128)S(1)}) custom-call(s32[1]{0:T(128)S(6)} %copy.10.flag_ref, bf16[640]{0:T(1024)(128)(2,1)} %gain_hbm.1, bf16[256,640]{1,0:T(8,128)(2,1)} %bitcast.7, bf16[256,640]{1,0:T(8,128)(2,1)} %bitcast.8, ...), custom_call_target="tpu_custom_call" | custom-call | tf_op jit(solution)/shard_map/layer_backward/pallas_call | solution.py:414
  57.3 1.5 %write_results.1 = (bf16[256,640]{1,0:T(8,128)(2,1)}, bf16[256,640]{1,0:T(8,128)(2,1)}, bf16[256,640]{1,0:T(8,128)(2,1)}, f32[640]{0:T(1024)}) custom-call(bf16[256,640]{1,0:T(8,128)(2,1)S(1)} %get-tuple-element.12.gq, bf16[256,640]{1,0:T(8,128)(2,1)S(1)} %get-tuple-element.13.gk, bf16[256,640]{1,0:T(8,128)(2,1)S(1)} %get-tuple-element.14.gv, ...), custom_call_target="tpu_custom_call" | custom-call | tf_op jit(solution)/shard_map/write_results/pallas_call | solution.py:426

commit v3 on v2

--- a/solution.py
+++ b/solution.py
@@ -13,6 +13,7 @@
 CHUNKS = tuple((h, h + 1) for h in range(HEADS))
 NC = len(CHUNKS)
 PIECES = 1
+STRAIGHT = (0,)
 F32, BF16 = jnp.float32, jnp.bfloat16
 
 
@@ -37,11 +38,11 @@
     flag_ref, gain_hbm, q_hbm, k_hbm, v_hbm, g_hbm,
     oq_ref, ok_ref, ov_ref, gg_ref,
     q_ref, k_ref, v_ref, g_ref, gain_ref,
-    x_st, y_st, r1, z_st, xr, w_st, yr, base, o_st, t_st, u_st, r2,
+    x_st, y_st, r1, z_st, xr, w_st, yr, base, o_st, t_st, u_st, r2, xo,
     attn, s_hi, s_lo, p_hi, p_lo, a_hi, a_lo, qt, up, gk_loc, gv_loc,
     sq, cr, inv_b, coef_b, zbuf, gcore, gx, gy, gdp,
-    in_sem, kv_sem, c1_s, c1_r, x1_s, x1_r, y_s, y_r, x2_s, x2_r, c2_s, c2_r,
-    z_s, z_r, gc_s, gc_r, gx_s, gx_r, gy_s, gy_r, gd_s, gd_r,
+    y_in, z2_in, z4_in, in_sem, kv_sem, c1_s, c1_r, x1_s, x1_r, y_s, y_r, x2_s, x2_r, c2_s, c2_r,
+    xo_s, xo_r, z_s, z_r, gc_s, gc_r, gx_s, gx_r, gy_s, gy_r, gd_s, gd_r,
 ):
     dp = lax.axis_index("dp")
     z = lax.axis_index("head")
@@ -76,10 +77,16 @@
 
     kv_loads = [load_head(0)]
     bar = pltpu.get_barrier_semaphore()
-    peers = [sibling] + [at(y, v, core) for v in xs] + [at(v, x, core) for v in ys]
-    peers += [{"head": v} for v in zs] + [{"dp": 1 - dp}]
+    def tell(sem, device):
+        pl.semaphore_signal(sem, inc=1, device_id=device, device_id_type=MESH)
+
+    def z_at(d):
+        return {"head": lax.rem(z + d + NZ, NZ)}
+
+    peers = [at(y, v, c) for v in xs for c in (core, 1 - core)] + [at(v, x, core) for v in (ys[0], ys[2])]
+    peers += [z_at(1), z_at(-1), {"dp": 1 - dp}, sibling]
     for p in peers:
-        pl.semaphore_signal(bar, inc=1, device_id=p, device_id_type=MESH)
+        tell(bar, p)
     kv_loads += [load_head(h) for h in range(1, HEADS)]
     loads = [load(*c, in_sem.at[i]) for i, c in enumerate(((q_hbm, q_ref), (g_hbm, g_ref), (gain_hbm, gain_ref)))]
 
@@ -87,7 +94,20 @@
     first0 = jnp.full((D, D), flag, jnp.int32) == 0
     low = jnp.full((D, D), core, jnp.int32) == 0
     causal = lax.broadcasted_iota(jnp.int32, (D, D), 0) >= lax.broadcasted_iota(jnp.int32, (D, D), 1)
-    sends = []
+    sends, late = [], []
+
+    def drain(copies):
+        for cp in copies:
+            cp.wait_send()
+        copies.clear()
+
+    def drain_y(copies):
+        for three in copies:
+            for e, cp in enumerate(three, 1):
+
+                @pl.when(sy + e < NY)
+                def _():
+                    cp.wait_send()
 
     def cols(h):
         return pl.ds(h * D, D)
@@ -107,6 +127,19 @@
 
     def stage_core(n, c):
         hs = pl.ds(CHUNKS[c][0], CHUNKS[c][1] - CHUNKS[c][0])
+        here = pl.ds(pl.multiple_of(x * PART, PART), PART)
+        if c in STRAIGHT:
+            out = []
+            for d, xx in enumerate(xs):
+                there = pl.ds(pl.multiple_of(xx * PART, PART), PART)
+                out.append(remote(x_st.at[n, hs, there], xr.at[n, sx, hs], x1_s.at[n, c, d], x1_r.at[n, c, d], at(y, xx, core)))
+                out.append(remote(y_st.at[n, hs, there], xo.at[n, NX - 1 - sx], xo_s.at[n, d], xo_r.at[n, d], at(y, xx, 1 - core)))
+            out.append(remote(y_st.at[n, hs, here], xo.at[n, NX - 1 - sx], xo_s.at[n, NX - 1], xo_r.at[n, NX - 1], sibling))
+            for cp in out:
+                cp.start()
+            xr[n, sx, hs] = x_st[n, hs, here]
+            sends.extend(out)
+            return out
         cp = remote(y_st.at[n, hs], r1.at[n, hs], c1_s.at[n, c], c1_r.at[n, c], sibling)
         cp.start()
         sends.append(cp)
@@ -114,6 +147,8 @@
 
     def stage_x(n, c, before):
         hs = pl.ds(CHUNKS[c][0], CHUNKS[c][1] - CHUNKS[c][0])
+        if c in STRAIGHT:
+            return before
         before.wait_recv()
         z_st[n, hs] = x_st[n, hs] + r1[n, hs]
         out = []
@@ -133,6 +168,9 @@
         hs = pl.ds(CHUNKS[c][0], CHUNKS[c][1] - CHUNKS[c][0])
         for cp in before:
             cp.wait_recv()
+        if c in STRAIGHT:
+            for t in range(NX):
+                xr[n, t, hs] += xo[n, t]
         w_st[n, hs] = (xr[n, 0, hs] + xr[n, 1, hs]) + (xr[n, 2, hs] + xr[n, 3, hs])
         out = []
         for e in (2, 1, 3):
@@ -179,7 +217,7 @@
         u_st[n, hs] = t_st[n, hs] + x_st[n, hs]
         cp = remote(u_st.at[n, hs], r2.at[n, hs], c2_s.at[n, c], c2_r.at[n, c], sibling)
         cp.start()
-        sends.append(cp)
+        late.append(cp)
         return cp
 
     def get_states(n, h, mask):
@@ -201,6 +239,9 @@
         heads(chunk, body)
         if c == 0:
             pl.semaphore_wait(bar, len(peers))
+            tell(y_in, at(ys[0], x, core))
+            tell(z2_in, z_at(1))
+            tell(z2_in, z_at(-1))
         c1.append(stage_core(0, c))
 
     def local_attn(h):
@@ -215,11 +256,16 @@
             attn[s, h] = mm(wide(hi, lo), tall(vv, vv), 1, 0)
 
     x1 = [stage_x(0, c, c1[c]) for c in range(NC)]
+    pl.semaphore_wait(y_in, 1)
     for cp in loads:
         cp.wait()
     gain = gain_ref[...].astype(F32).reshape(1, HEADS * D)
     heads((0, 2), local_attn)
     yy = [stage_y(0, c, x1[c]) for c in range(NC)]
+    pl.semaphore_wait(z2_in, 2)
+    tell(z4_in, z_at(2))
+    tell(z4_in, z_at(2))
+    tell(z4_in, z_at(-2))
     heads((2, 5), local_attn)
     x2 = [stage_back(0, c, yy[c]) for c in range(NC)]
     c2 = [stage_swap(0, c, x2[c]) for c in range(NC)]
@@ -247,12 +293,16 @@
 
     zero = jnp.zeros((8 - 4, D), F32)
     zbuf[z] = tall(*[jnp.sum(jnp.transpose(m), axis=0, keepdims=True) for m in (sq[0], sq[1], cr[0], cr[1])], zero)
+    pl.semaphore_wait(z4_in, 3)
     zc = []
     for d, zz in enumerate(zs):
         cp = remote(zbuf.at[z], zbuf.at[z], z_s.at[d], z_r.at[d], {"head": zz})
         cp.start()
         zc.append(cp)
-    sends.extend(zc)
+    drain(sends)
+    drain(late)
+    drain_y(yy)
+    late.extend(zc)
     for cp in zc:
         cp.wait_recv()
     sums = zbuf[0]
@@ -308,7 +358,7 @@
             cp = remote(buf.at[me], buf.at[me], ssem.at[d], rsem.at[d], device)
             cp.start()
             out.append(cp)
-        sends.extend(out)
+        late.extend(out)
         return out
 
     def gain_sum(buf, count, copies):
@@ -327,11 +377,14 @@
     gx[x] = gain_sum(gcore, 2, gc)
     gc = gain_send(gx, x, gx_s, gx_r, [at(y, v, core) for v in xs])
     heads((2, 4), local_grads)
+    drain(sends)
     x2 = [stage_back(1, c, yy[c]) for c in range(NC)]
     gy[y] = gain_sum(gx, NX, gc)
     gc = gain_send(gy, y, gy_s, gy_r, [at(v, x, core) for v in ys])
     heads((4, 5), local_grads)
+    drain_y(yy)
     c2 = [stage_swap(1, c, x2[c]) for c in range(NC)]
+    drain(sends)
     gdp[dp] = gain_sum(gy, NY, gc)
     gc = gain_send(gdp, dp, gd_s, gd_r, [{"dp": 1 - dp}])
 
@@ -351,18 +404,7 @@
         heads(chunk, body)
     gg_ref[...] = gain_sum(gdp, 2, gc)
 
-    for cp in sends:
-        cp.wait_send()
-    for n in range(2):
-        for c, chunk in enumerate(CHUNKS):
-            hs = pl.ds(chunk[0], chunk[1] - chunk[0])
-            for e in range(1, NY):
-
-                @pl.when(sy + e < NY)
-                def _():
-                    remote(
-                        w_st.at[n, hs], yr.at[n, e - 1, hs], y_s.at[n, c, e - 1], y_r.at[n, c, e - 1], sibling
-                    ).wait_send()
+    drain(late)
 
 
 def write_kernel(gq, gk, gv, gg, oq, ok, ov, og, sem):
@@ -396,14 +438,16 @@
         pltpu.VMEM((2, NX) + piece, F32),
     ]
     scratch += [pltpu.VMEM(state, F32)] * 3
+    scratch += [pltpu.VMEM((2, NX, 1, PART, D), F32)]
     scratch += [pltpu.VMEM(state, F32)]
     scratch += [pltpu.VMEM(state, BF16)] * 7
     scratch += [pltpu.VMEM(state, F32)] * 3
     scratch += [pltpu.VMEM((2, D, D), F32)] * 4
     scratch += [pltpu.VMEM((n, 8, D), F32) for n in (NZ, 2, NX, NY, 2)]
-    scratch += [dma((3,)), dma((2, HEADS))]
+    scratch += [pltpu.SemaphoreType.REGULAR] * 3 + [dma((3,)), dma((2, HEADS))]
     for shape_of in ((2, NC), (2, NC, NX - 1), (2, NC, NY - 1), (2, NC, NX - 1), (2, NC)):
         scratch += [dma(shape_of)] * 2
+    scratch += [dma((2, NX))] * 2
     for count in (NZ - 1, 1, NX - 1, NY - 1, 1):
         scratch += [dma((count,))] * 2
     hbm = pl.BlockSpec(memory_space=pl.ANY)

time: 59 us -> 56.5 us (0.958)
  the two profiles are of different devices: /device:TPU:8 before, /device:TPU:1 now
where the time goes in v3:
time: 56.5 us; the launch traced here: 55.8 us
  Pallas kernels  54.5 us (96%)
  between operations  1.29 us (2%)
    pallas_call x1, Pallas kernels, shards(): pl.pallas_call(kernel, name='layer_backward', out_shape=(inner, inner, in...  53 us
    pallas_call x1, Pallas kernels, shards(): pl.pallas_call(write_kernel, name='write_results', out_shape=(out, out, o...  1.55 us

profile of v3, /device:TPU:1, one launch (start us, length us, event | category | flops | bytes accessed | tf_op | source)
XLA Modules:
  0.0 55.8 jit_solution(11694908191303144480)
XLA Ops:
  1.3 53.0 %layer_backward.1 = (bf16[256,640]{1,0:T(8,128)(2,1)S(1)}, bf16[256,640]{1,0:T(8,128)(2,1)S(1)}, bf16[256,640]{1,0:T(8,128)(2,1)S(1)}, f32[8,128]{1,0:T(8,128)S(1)}) custom-call(s32[1]{0:T(128)S(6)} %copy.10.flag_ref, bf16[640]{0:T(1024)(128)(2,1)} %gain_hbm.1, bf16[256,640]{1,0:T(8,128)(2,1)} %bitcast.7, bf16[256,640]{1,0:T(8,128)(2,1)} %bitcast.8, ...), custom_call_target="tpu_custom_call" | custom-call | tf_op jit(solution)/shard_map/layer_backward/pallas_call | solution.py:458
  54.3 1.5 %write_results.1 = (bf16[256,640]{1,0:T(8,128)(2,1)}, bf16[256,640]{1,0:T(8,128)(2,1)}, bf16[256,640]{1,0:T(8,128)(2,1)}, f32[640]{0:T(1024)}) custom-call(bf16[256,640]{1,0:T(8,128)(2,1)S(1)} %get-tuple-element.12.gq, bf16[256,640]{1,0:T(8,128)(2,1)S(1)} %get-tuple-element.13.gk, bf16[256,640]{1,0:T(8,128)(2,1)S(1)} %get-tuple-element.14.gv, ...), custom_call_target="tpu_custom_call" | custom-call | tf_op jit(solution)/shard_map/write_results/pallas_call | solution.py:470

commit v4 on v3

--- a/solution.py
+++ b/solution.py
@@ -10,9 +10,8 @@
 NX, NY, NZ = 4, 4, 8
 HEADS = 5
 PART = D // NX
-CHUNKS = tuple((h, h + 1) for h in range(HEADS))
+CHUNKS = tuple((h, 0, PART) for h in range(HEADS))
 NC = len(CHUNKS)
-PIECES = 1
 STRAIGHT = (0,)
 F32, BF16 = jnp.float32, jnp.bfloat16
 
@@ -38,7 +37,7 @@
     flag_ref, gain_hbm, q_hbm, k_hbm, v_hbm, g_hbm,
     oq_ref, ok_ref, ov_ref, gg_ref,
     q_ref, k_ref, v_ref, g_ref, gain_ref,
-    x_st, y_st, r1, z_st, xr, w_st, yr, base, o_st, t_st, u_st, r2, xo,
+    x_st, y_st, r1, z_st, xr, w_st, yr, o_st, t_st, u_st, r2, xo,
     attn, s_hi, s_lo, p_hi, p_lo, a_hi, a_lo, qt, up, gk_loc, gv_loc,
     sq, cr, inv_b, coef_b, zbuf, gcore, gx, gy, gdp,
     y_in, z2_in, z4_in, in_sem, kv_sem, c1_s, c1_r, x1_s, x1_r, y_s, y_r, x2_s, x2_r, c2_s, c2_r,
@@ -76,6 +75,7 @@
         return [load(src.at[where], dst.at[where], kv_sem.at[i, h]) for i, (src, dst) in enumerate(((k_hbm, k_ref), (v_hbm, v_ref)))]
 
     kv_loads = [load_head(0)]
+    yr[...] = jnp.zeros_like(yr)
     bar = pltpu.get_barrier_semaphore()
     def tell(sem, device):
         pl.semaphore_signal(sem, inc=1, device_id=device, device_id_type=MESH)
@@ -119,63 +119,62 @@
         for h in range(*chunk):
             body(h)
 
+    def piece(c):
+        h, r0, r1 = CHUNKS[c]
+        return h, pl.ds(r0, r1 - r0)
+
     def put_state(n, h, s0, s1, mask):
         first = jnp.where(mask, s0, s1)
         both = s0 + s1
-        x_st[n, h] = jnp.where(low, first, both)
-        y_st[n, h] = jnp.where(low, both, first)
+        x_st[n, h] = jnp.where(low, first, both).reshape(NX, PART, D)
+        y_st[n, h] = jnp.where(low, both, first).reshape(NX, PART, D)
 
     def stage_core(n, c):
-        hs = pl.ds(CHUNKS[c][0], CHUNKS[c][1] - CHUNKS[c][0])
-        here = pl.ds(pl.multiple_of(x * PART, PART), PART)
+        h, rr = piece(c)
         if c in STRAIGHT:
             out = []
             for d, xx in enumerate(xs):
-                there = pl.ds(pl.multiple_of(xx * PART, PART), PART)
-                out.append(remote(x_st.at[n, hs, there], xr.at[n, sx, hs], x1_s.at[n, c, d], x1_r.at[n, c, d], at(y, xx, core)))
-                out.append(remote(y_st.at[n, hs, there], xo.at[n, NX - 1 - sx], xo_s.at[n, d], xo_r.at[n, d], at(y, xx, 1 - core)))
-            out.append(remote(y_st.at[n, hs, here], xo.at[n, NX - 1 - sx], xo_s.at[n, NX - 1], xo_r.at[n, NX - 1], sibling))
+                out.append(remote(x_st.at[n, h, xx, rr], xr.at[n, sx, h, rr], x1_s.at[n, c, d], x1_r.at[n, c, d], at(y, xx, core)))
+                out.append(remote(y_st.at[n, h, xx, rr], xo.at[n, NX - 1 - sx, rr], xo_s.at[n, c, d], xo_r.at[n, c, d], at(y, xx, 1 - core)))
+            d = NX - 1
+            out.append(remote(y_st.at[n, h, x, rr], xo.at[n, NX - 1 - sx, rr], xo_s.at[n, c, d], xo_r.at[n, c, d], sibling))
             for cp in out:
                 cp.start()
-            xr[n, sx, hs] = x_st[n, hs, here]
+            xr[n, sx, h, rr] = x_st[n, h, x, rr]
             sends.extend(out)
             return out
-        cp = remote(y_st.at[n, hs], r1.at[n, hs], c1_s.at[n, c], c1_r.at[n, c], sibling)
+        cp = remote(y_st.at[n, h, :, rr], r1.at[n, h, :, rr], c1_s.at[n, c], c1_r.at[n, c], sibling)
         cp.start()
         sends.append(cp)
         return cp
 
     def stage_x(n, c, before):
-        hs = pl.ds(CHUNKS[c][0], CHUNKS[c][1] - CHUNKS[c][0])
+        h, rr = piece(c)
         if c in STRAIGHT:
             return before
         before.wait_recv()
-        z_st[n, hs] = x_st[n, hs] + r1[n, hs]
+        z_st[n, h, :, rr] = x_st[n, h, :, rr] + r1[n, h, :, rr]
         out = []
         for d, xx in enumerate(xs):
-            there = pl.multiple_of(xx * PART, PART)
-            cp = remote(
-                z_st.at[n, hs, pl.ds(there, PART)], xr.at[n, sx, hs], x1_s.at[n, c, d], x1_r.at[n, c, d],
-                at(y, xx, core),
-            )
+            cp = remote(z_st.at[n, h, xx, rr], xr.at[n, sx, h, rr], x1_s.at[n, c, d], x1_r.at[n, c, d], at(y, xx, core))
             cp.start()
             out.append(cp)
-        xr[n, sx, hs] = z_st[n, hs, pl.ds(pl.multiple_of(x * PART, PART), PART)]
+        xr[n, sx, h, rr] = z_st[n, h, x, rr]
         sends.extend(out)
         return out
 
     def stage_y(n, c, before):
-        hs = pl.ds(CHUNKS[c][0], CHUNKS[c][1] - CHUNKS[c][0])
+        h, rr = piece(c)
         for cp in before:
             cp.wait_recv()
         if c in STRAIGHT:
             for t in range(NX):
-                xr[n, t, hs] += xo[n, t]
-        w_st[n, hs] = (xr[n, 0, hs] + xr[n, 1, hs]) + (xr[n, 2, hs] + xr[n, 3, hs])
+                xr[n, t, h, rr] += xo[n, t, rr]
+        w_st[n, h, rr] = (xr[n, 0, h, rr] + xr[n, 1, h, rr]) + (xr[n, 2, h, rr] + xr[n, 3, h, rr])
         out = []
         for e in (2, 1, 3):
             yy = jnp.where(core == 0, lax.rem(y + e, NY), lax.rem(y + NY - e, NY))
-            cp = remote(w_st.at[n, hs], yr.at[n, e - 1, hs], y_s.at[n, c, e - 1], y_r.at[n, c, e - 1], at(yy, x, core))
+            cp = remote(w_st.at[n, h, rr], yr.at[n, e - 1, h, rr], y_s.at[n, c, e - 1], y_r.at[n, c, e - 1], at(yy, x, core))
 
             @pl.when(sy + e < NY)
             def _():
@@ -185,58 +184,48 @@
         return [out[1], out[0], out[2]]
 
     def stage_back(n, c, before):
-        hs = pl.ds(CHUNKS[c][0], CHUNKS[c][1] - CHUNKS[c][0])
-        base[n, hs] = jnp.zeros_like(base[n, hs])
+        h, rr = piece(c)
         for e, cp in enumerate(before, 1):
-
-            @pl.when(sy >= e)
-            def _():
-                cp.wait_recv()
-                base[n, hs] += yr[n, e - 1, hs]
-
-        total = base[n, hs]
+            pl.when(sy >= e)(cp.wait_recv)
+        total = (yr[n, 0, h, rr] + yr[n, 1, h, rr]) + yr[n, 2, h, rr]
         for t in range(NX):
-            o_st[n, t, hs] = total
+            o_st[n, t, h, rr] = total
             if t < NX - 1:
-                total = total + xr[n, t, hs]
+                total = total + xr[n, t, h, rr]
         out = []
-        here = pl.ds(pl.multiple_of(x * PART, PART), PART)
         for d, xx in enumerate(xs):
             t = jnp.where(core == 0, xx, NX - 1 - xx)
-            cp = remote(o_st.at[n, t, hs], t_st.at[n, hs, here], x2_s.at[n, c, d], x2_r.at[n, c, d], at(y, xx, core))
+            cp = remote(o_st.at[n, t, h, rr], t_st.at[n, h, x, rr], x2_s.at[n, c, d], x2_r.at[n, c, d], at(y, xx, core))
             cp.start()
             out.append(cp)
-        t_st[n, hs, here] = o_st[n, sx, hs]
+        t_st[n, h, x, rr] = o_st[n, sx, h, rr]
         sends.extend(out)
         return out
 
     def stage_swap(n, c, before):
-        hs = pl.ds(CHUNKS[c][0], CHUNKS[c][1] - CHUNKS[c][0])
+        h, rr = piece(c)
         for cp in before:
             cp.wait_recv()
-        u_st[n, hs] = t_st[n, hs] + x_st[n, hs]
-        cp = remote(u_st.at[n, hs], r2.at[n, hs], c2_s.at[n, c], c2_r.at[n, c], sibling)
+        u_st[n, h, :, rr] = t_st[n, h, :, rr] + x_st[n, h, :, rr]
+        cp = remote(u_st.at[n, h, :, rr], r2.at[n, h, :, rr], c2_s.at[n, c], c2_r.at[n, c], sibling)
         cp.start()
         late.append(cp)
         return cp
 
     def get_states(n, h, mask):
-        mine, other = t_st[n, h], r2[n, h]
-        own_first = jnp.where(low, x_st[n, h], y_st[n, h])
+        mine, other = t_st[n, h].reshape(D, D), r2[n, h].reshape(D, D)
+        own_first = jnp.where(low, x_st[n, h].reshape(D, D), y_st[n, h].reshape(D, D))
         first = jnp.where(low, mine, other)
         second = (mine + other) + own_first
         return jnp.where(mask, first, second), jnp.where(mask, second, first)
 
     c1 = []
-    for c, chunk in enumerate(CHUNKS):
-
-        def body(h):
+    for c, (h, r0, _) in enumerate(CHUNKS):
+        if r0 == 0:
             for cp in kv_loads[h]:
                 cp.wait()
             kv = [mm(k_ref[rows(s), cols(h)], v_ref[rows(s), cols(h)], 0, 0) for s in range(2)]
             put_state(0, h, kv[0], kv[1], first0)
-
-        heads(chunk, body)
         if c == 0:
             pl.semaphore_wait(bar, len(peers))
             tell(y_in, at(ys[0], x, core))
@@ -270,8 +259,10 @@
     x2 = [stage_back(0, c, yy[c]) for c in range(NC)]
     c2 = [stage_swap(0, c, x2[c]) for c in range(NC)]
 
-    for c, chunk in enumerate(CHUNKS):
-        c2[c].wait_recv()
+    for h in range(HEADS):
+        for c, chunk in enumerate(CHUNKS):
+            if chunk[0] == h:
+                c2[c].wait_recv()
 
         def body(h):
             prefix = get_states(0, h, first0)
@@ -289,7 +280,7 @@
                     sq[s] += a * a
                     cr[s] += up[s, h] * a
 
-        heads(chunk, body)
+        body(h)
 
     zero = jnp.zeros((8 - 4, D), F32)
     zbuf[z] = tall(*[jnp.sum(jnp.transpose(m), axis=0, keepdims=True) for m in (sq[0], sq[1], cr[0], cr[1])], zero)
@@ -302,7 +293,7 @@
     drain(sends)
     drain(late)
     drain_y(yy)
-    late.extend(zc)
+    sends.extend(zc)
     for cp in zc:
         cp.wait_recv()
     sums = zbuf[0]
@@ -317,7 +308,7 @@
 
     last0 = jnp.logical_not(first0)
     c1 = []
-    for c, chunk in enumerate(CHUNKS):
+    for c, (h, r0, _) in enumerate(CHUNKS):
 
         def body(h):
             adj = []
@@ -329,7 +320,8 @@
                 adj.append(mm(wide(qq, qq), tall(hi, lo), 1, 0))
             put_state(1, h, adj[0], adj[1], last0)
 
-        heads(chunk, body)
+        if r0 == 0:
+            body(h)
         c1.append(stage_core(1, c))
 
     def local_grads(h):
@@ -358,7 +350,7 @@
             cp = remote(buf.at[me], buf.at[me], ssem.at[d], rsem.at[d], device)
             cp.start()
             out.append(cp)
-        late.extend(out)
+        sends.extend(out)
         return out
 
     def gain_sum(buf, count, copies):
@@ -373,23 +365,25 @@
     gcore[core] = gain_terms()
     gc = gain_send(gcore, core, gc_s, gc_r, [sibling])
     heads((0, 2), local_grads)
-    yy = [stage_y(1, c, x1[c]) for c in range(NC)]
     gx[x] = gain_sum(gcore, 2, gc)
     gc = gain_send(gx, x, gx_s, gx_r, [at(y, v, core) for v in xs])
+    yy = [stage_y(1, c, x1[c]) for c in range(NC)]
+    gy[y] = gain_sum(gx, NX, gc)
+    gc = gain_send(gy, y, gy_s, gy_r, [at(v, x, core) for v in ys])
     heads((2, 4), local_grads)
     drain(sends)
     x2 = [stage_back(1, c, yy[c]) for c in range(NC)]
-    gy[y] = gain_sum(gx, NX, gc)
-    gc = gain_send(gy, y, gy_s, gy_r, [at(v, x, core) for v in ys])
+    gdp[dp] = gain_sum(gy, NY, gc)
+    gc = gain_send(gdp, dp, gd_s, gd_r, [{"dp": 1 - dp}])
     heads((4, 5), local_grads)
     drain_y(yy)
     c2 = [stage_swap(1, c, x2[c]) for c in range(NC)]
     drain(sends)
-    gdp[dp] = gain_sum(gy, NY, gc)
-    gc = gain_send(gdp, dp, gd_s, gd_r, [{"dp": 1 - dp}])
-
-    for c, chunk in enumerate(CHUNKS):
-        c2[c].wait_recv()
+
+    for h in range(HEADS):
+        for c, chunk in enumerate(CHUNKS):
+            if chunk[0] == h:
+                c2[c].wait_recv()
 
         def body(h):
             suffix = get_states(1, h, last0)
@@ -401,21 +395,19 @@
                 ok_ref[rows(s), cols(h)] = gk.astype(BF16)
                 ov_ref[rows(s), cols(h)] = gv.astype(BF16)
 
-        heads(chunk, body)
+        body(h)
     gg_ref[...] = gain_sum(gdp, 2, gc)
 
     drain(late)
 
 
-def write_kernel(gq, gk, gv, gg, oq, ok, ov, og, sem):
-    copies = []
-    for i, (src, dst) in enumerate(((gq, oq), (gk, ok), (gv, ov))):
-        for j in range(PIECES):
-            rows = pl.ds(j * (src.shape[0] // PIECES), src.shape[0] // PIECES)
-            copies.append(pltpu.make_async_copy(src.at[rows], dst.at[rows], sem.at[i, j]))
-            copies[-1].start()
+def write_kernel(gq, gk, gv, gg, oq, ok, ov, og, line, sem):
+    copies = [pltpu.make_async_copy(src, dst, sem.at[i]) for i, (src, dst) in enumerate(((gq, oq), (gk, ok), (gv, ov), (line, og)))]
+    for cp in copies[:3]:
+        cp.start()
     for h in range(HEADS):
-        og[pl.ds(h * D, D)] = gg[h]
+        line[pl.ds(h * D, D)] = gg[h]
+    copies[3].start()
     for cp in copies:
         cp.wait()
 
@@ -426,19 +418,19 @@
     flat = [a.reshape(tokens, width) for a in (queries, keys, values, grad_out)]
     gain = pltpu.with_memory_space_constraint(gain, pltpu.HBM)
     state = (2, HEADS, D, D)
+    quarters = (2, HEADS, NX, PART, D)
     piece = (HEADS, PART, D)
     dma = pltpu.SemaphoreType.DMA
     scratch = [pltpu.VMEM((tokens, width), BF16)] * 4 + [pltpu.VMEM((width,), BF16)]
-    scratch += [pltpu.VMEM(state, F32)] * 4
+    scratch += [pltpu.VMEM(quarters, F32)] * 4
     scratch += [
         pltpu.VMEM((2, NX) + piece, F32),
         pltpu.VMEM((2,) + piece, F32),
         pltpu.VMEM((2, NY - 1) + piece, F32),
-        pltpu.VMEM((2,) + piece, F32),
         pltpu.VMEM((2, NX) + piece, F32),
     ]
-    scratch += [pltpu.VMEM(state, F32)] * 3
-    scratch += [pltpu.VMEM((2, NX, 1, PART, D), F32)]
+    scratch += [pltpu.VMEM(quarters, F32)] * 3
+    scratch += [pltpu.VMEM((2, NX, PART, D), F32)]
     scratch += [pltpu.VMEM(state, F32)]
     scratch += [pltpu.VMEM(state, BF16)] * 7
     scratch += [pltpu.VMEM(state, F32)] * 3
@@ -447,7 +439,7 @@
     scratch += [pltpu.SemaphoreType.REGULAR] * 3 + [dma((3,)), dma((2, HEADS))]
     for shape_of in ((2, NC), (2, NC, NX - 1), (2, NC, NY - 1), (2, NC, NX - 1), (2, NC)):
         scratch += [dma(shape_of)] * 2
-    scratch += [dma((2, NX))] * 2
+    scratch += [dma((2, len(STRAIGHT), NX))] * 2
     for count in (NZ - 1, 1, NX - 1, NY - 1, 1):
         scratch += [dma((count,))] * 2
     hbm = pl.BlockSpec(memory_space=pl.ANY)
@@ -458,7 +450,7 @@
     gq, gk, gv, gg = pl.pallas_call(
         kernel,
         name="layer_backward",
-        out_shape=(inner, inner, inner, jax.ShapeDtypeStruct((8, D), F32)),
+        out_shape=(inner, inner, inner, pltpu.VMEM((8, D), F32)),
         in_specs=[pl.BlockSpec(memory_space=pltpu.SMEM), hbm, hbm, hbm, hbm, hbm],
         out_specs=(vmem, vmem, vmem, vmem),
         scratch_shapes=scratch,
@@ -466,16 +458,16 @@
             collective_id=0, has_side_effects=True, vmem_limit_bytes=32 * 1024 * 1024
         ),
     )(order_flag, gain, *flat)
-    gq, gk, gv = [pltpu.with_memory_space_constraint(a, pltpu.VMEM) for a in (gq, gk, gv)]
+    results = [pltpu.with_memory_space_constraint(a, pltpu.VMEM) for a in (gq, gk, gv, gg)]
     gq, gk, gv, gg = pl.pallas_call(
         write_kernel,
         name="write_results",
         out_shape=(out, out, out, jax.ShapeDtypeStruct((width,), F32)),
         in_specs=[vmem, vmem, vmem, vmem],
-        out_specs=(hbm, hbm, hbm, vmem),
-        scratch_shapes=[dma((3, PIECES))],
+        out_specs=(hbm, hbm, hbm, hbm),
+        scratch_shapes=[pltpu.VMEM((width,), F32), dma((4,))],
         compiler_params=pltpu.CompilerParams(vmem_limit_bytes=32 * 1024 * 1024),
-    )(gq, gk, gv, gg)
+    )(*results)
     return gq.reshape(shape), gk.reshape(shape), gv.reshape(shape), gg
 
 

time: 56.5 us -> 54.9 us (0.972)
  Pallas kernels: 54.5 us -> 53.4 us
    pallas_call x1, Pallas kernels: 1.55 us -> 0.98 us  [shards(): pl.pallas_call(write_kernel, name='write_results', out_shape=(out, out, o...]
where the time goes in v4:
time: 54.9 us; the launch traced here: 54.7 us
  Pallas kernels  53.4 us (97%)
  between operations  1.29 us (2%)
    pallas_call x1, Pallas kernels, shards(): pl.pallas_call(kernel, name='layer_backward', out_shape=(inner, inner, in...  52.5 us

profile of v4, /device:TPU:1, one launch (start us, length us, event | category | flops | bytes accessed | tf_op | source)
XLA Modules:
  0.0 54.7 jit_solution(5612338351916319617)
XLA Ops:
  1.3 52.5 %layer_backward.1 = (bf16[256,640]{1,0:T(8,128)(2,1)S(1)}, bf16[256,640]{1,0:T(8,128)(2,1)S(1)}, bf16[256,640]{1,0:T(8,128)(2,1)S(1)}, f32[8,128]{1,0:T(8,128)S(1)}) custom-call(s32[1]{0:T(128)S(6)} %copy.10.flag_ref, bf16[640]{0:T(1024)(128)(2,1)} %gain_hbm.1, bf16[256,640]{1,0:T(8,128)(2,1)} %bitcast.7, bf16[256,640]{1,0:T(8,128)(2,1)} %bitcast.8, ...), custom_call_target="tpu_custom_call" | custom-call | tf_op jit(solution)/shard_map/layer_backward/pallas_call | solution.py:450
  53.7 1.0 %write_results.1 = (bf16[256,640]{1,0:T(8,128)(2,1)}, bf16[256,640]{1,0:T(8,128)(2,1)}, bf16[256,640]{1,0:T(8,128)(2,1)}, f32[640]{0:T(1024)}) custom-call(bf16[256,640]{1,0:T(8,128)(2,1)S(1)} %get-tuple-element.12.gq, bf16[256,640]{1,0:T(8,128)(2,1)S(1)} %get-tuple-element.13.gk, bf16[256,640]{1,0:T(8,128)(2,1)S(1)} %get-tuple-element.14.gv, ...), custom_call_target="tpu_custom_call" | custom-call | tf_op jit(solution)/shard_map/write_results/pallas_call | solution.py:462

commit v5 on v4

v5 whole, which is shorter than its diff:
```python
import jax
import jax.numpy as jnp
from jax import lax
from jax.experimental import pallas as pl
from jax.experimental.pallas import tpu as pltpu
from jax.sharding import PartitionSpec as P

MESH = pl.DeviceIdType.MESH
D = 128
NX, NY, NZ = 4, 4, 8
HEADS = 5
PART = D // NX
F32, BF16 = jnp.float32, jnp.bfloat16


def mm(a, b, ca, cb):
    return lax.dot_general(a, b, (((ca,), (cb,)), ((), ())), preferred_element_type=F32)


def parts(x):
    hi = x.astype(BF16)
    return hi, (x - hi.astype(F32)).astype(BF16)


def wide(*a):
    return jnp.concatenate(a, axis=1)


def tall(*a):
    return jnp.concatenate(a, axis=0)


def kernel(
    flag_ref, gain_hbm, q_hbm, k_hbm, v_hbm, g_hbm,
    oq_ref, ok_ref, ov_ref, gg_ref,
    q_ref, k_ref, v_ref, g_ref, gain_ref, gain_rows,
    x_st, y_st, r1, z_st, xr, w_st, yr, o_st, t_st, u_st, r2, xo,
    attn, s_hi, s_lo, p_hi, p_lo, a_hi, a_lo, qt, up, gk_loc, gv_loc,
    sq, cr, inv_b, coef_b, zbuf, gcore, gx, gy, gdp,
    y_in, z2_in, z4_in, in_sem, kv_sem, c1_s, c1_r, x1_s, x1_r, y_s, y_r, x2_s, x2_r, c2_s, c2_r,
    xo_s, xo_r, z_s, z_r, gc_s, gc_r, gx_s, gx_r, gy_s, gy_r, gd_s, gd_r,
):
    dp = lax.axis_index("dp")
    z = lax.axis_index("head")
    ctx = lax.axis_index("ctx")
    core = lax.rem(ctx, 2)
    x = lax.rem(ctx // 2, NX)
    y = ctx // (2 * NX)
    sx = jnp.where(core == 0, x, NX - 1 - x)
    sy = jnp.where(core == 0, y, NY - 1 - y)

    def at(yy, xx, cc):
        return {"ctx": (yy * NX + xx) * 2 + cc}

    sibling = at(y, x, 1 - core)
    xs = [lax.rem(x + d, NX) for d in (2, 1, 3)]
    ys = [lax.rem(y + d, NY) for d in range(1, NY)]
    zs = [lax.rem(z + d, NZ) for d in range(1, NZ)]
    bar = pltpu.get_barrier_semaphore()

    def remote(src, dst, ssem, rsem, device):
        return pltpu.make_async_remote_copy(
            src_ref=src, dst_ref=dst, send_sem=ssem, recv_sem=rsem, device_id=device, device_id_type=MESH
        )

    def start(copies):
        for cp in copies:
            cp.start()

    def received(copies):
        for cp in copies:
            cp.wait_recv()

    def sent(copies):
        for cp in copies:
            cp.wait_send()

    def loop(first, last, body):
        def step(h, carry):
            body(h)
            return carry

        lax.fori_loop(first, last, step, 0)

    def cols(h):
        return pl.ds(pl.multiple_of(h * D, D), D)

    def rows(s):
        return pl.ds(s * D, D)

    def tell(sem, device):
        pl.semaphore_signal(sem, inc=1, device_id=device, device_id_type=MESH)

    def z_at(d):
        return {"head": lax.rem(z + d + NZ, NZ)}

    def kv_loads(h):
        where = (slice(None), cols(h))
        pairs = ((k_hbm, k_ref), (v_hbm, v_ref))
        return [pltpu.make_async_copy(src.at[where], dst.at[where], kv_sem.at[i, h]) for i, (src, dst) in enumerate(pairs)]

    pairs = ((q_hbm, q_ref), (g_hbm, g_ref), (gain_hbm, gain_ref))
    loads = [pltpu.make_async_copy(src, dst, in_sem.at[i]) for i, (src, dst) in enumerate(pairs)]
    start(kv_loads(0))
    yr[...] = jnp.zeros_like(yr)
    peers = [at(y, v, c) for v in xs for c in (core, 1 - core)] + [at(v, x, core) for v in (ys[0], ys[2])]
    peers += [z_at(1), z_at(-1), {"dp": 1 - dp}, sibling]
    for p in peers:
        tell(bar, p)
    loop(1, HEADS, lambda h: start(kv_loads(h)))
    start(loads)

    first0 = jnp.full((D, D), flag_ref[0], jnp.int32) == 0
    last0 = jnp.logical_not(first0)
    low = jnp.full((D, D), core, jnp.int32) == 0
    causal = lax.broadcasted_iota(jnp.int32, (D, D), 0) >= lax.broadcasted_iota(jnp.int32, (D, D), 1)

    def core_copy(n, h):
        return remote(y_st.at[n, h], r1.at[n, h], c1_s.at[n, h], c1_r.at[n, h], sibling)

    def x_copies(n, h, src):
        return [
            remote(src.at[n, h, xx], xr.at[n, sx, h], x1_s.at[n, h], x1_r.at[n, h], at(y, xx, core))
            for xx in xs
        ]

    def straight_copies(n):
        to = [(xx, at(y, xx, 1 - core)) for xx in xs] + [(x, sibling)]
        return [
            remote(y_st.at[n, 0, xx], xo.at[n, NX - 1 - sx], xo_s.at[n], xo_r.at[n], device)
            for xx, device in to
        ]

    def y_copies(n, h):
        out = []
        for e in range(1, NY):
            yy = jnp.where(core == 0, lax.rem(y + e, NY), lax.rem(y + NY - e, NY))
            out.append(
                remote(w_st.at[n, h], yr.at[n, e - 1, h], y_s.at[n, h, e - 1], y_r.at[n, h, e - 1], at(yy, x, core))
            )
        return out

    def back_copies(n, h):
        out = []
        for xx in xs:
            t = jnp.where(core == 0, xx, NX - 1 - xx)
            out.append(remote(o_st.at[n, t, h], t_st.at[n, h, x], x2_s.at[n, h], x2_r.at[n, h], at(y, xx, core)))
        return out

    def x_all(n, h):
        three = xr.at[n, pl.ds(0, NX - 1), h]
        return remote(three, three, x1_s.at[n, h], x1_r.at[n, h], sibling)

    def straight_all(n):
        return remote(xo.at[n], xo.at[n], xo_s.at[n], xo_r.at[n], sibling)

    def back_all(n, h):
        three = t_st.at[n, h, pl.ds(0, NX - 1)]
        return remote(three, three, x2_s.at[n, h], x2_r.at[n, h], sibling)

    def swap_copy(n, h):
        return remote(u_st.at[n, h], r2.at[n, h], c2_s.at[n, h], c2_r.at[n, h], sibling)

    def put_state(n, h, s0, s1, mask):
        first = jnp.where(mask, s0, s1)
        both = s0 + s1
        x_st[n, h] = jnp.where(low, first, both).reshape(NX, PART, D)
        y_st[n, h] = jnp.where(low, both, first).reshape(NX, PART, D)

    def stage_straight(n):
        for a, b in zip(x_copies(n, 0, x_st), straight_copies(n)):
            a.start()
            b.start()
        straight_copies(n)[-1].start()
        xr[n, sx, 0] = x_st[n, 0, x]

    def stage_x(n, h):
        core_copy(n, h).wait_recv()
        z_st[n, h] = x_st[n, h] + r1[n, h]
        start(x_copies(n, h, z_st))
        xr[n, sx, h] = z_st[n, h, x]

    def stage_y(n, h):
        x_all(n, h).wait_recv()
        w_st[n, h] = (xr[n, 0, h] + xr[n, 1, h]) + (xr[n, 2, h] + xr[n, 3, h])
        copies = y_copies(n, h)
        for e in (2, 1, 3):
            pl.when(sy + e < NY)(copies[e - 1].start)

    def stage_y_straight(n):
        received([x_all(n, 0), straight_all(n)])
        total = None
        for t in range(NX):
            term = xr[n, t, 0] + xo[n, t]
            xr[n, t, 0] = term
            total = term if total is None else total + term
        w_st[n, 0] = total
        copies = y_copies(n, 0)
        for e in (2, 1, 3):
            pl.when(sy + e < NY)(copies[e - 1].start)

    def stage_back(n, h):
        for e, cp in enumerate(y_copies(n, h), 1):
            pl.when(sy >= e)(cp.wait_recv)
        total = (yr[n, 0, h] + yr[n, 1, h]) + yr[n, 2, h]
        for t in range(NX):
            o_st[n, t, h] = total
            if t < NX - 1:
                total = total + xr[n, t, h]
        start(back_copies(n, h))
        t_st[n, h, x] = o_st[n, sx, h]

    def stage_swap(n, h):
        back_all(n, h).wait_recv()
        u_st[n, h] = t_st[n, h] + x_st[n, h]
        swap_copy(n, h).start()

    def drain_first(n):
        sent([x_all(n, 0), straight_all(n)])

        def body(h):
            sent([core_copy(n, h), x_all(n, h)])

        loop(1, HEADS, body)

    def drain_y(n):
        def body(h):
            for e, cp in enumerate(y_copies(n, h), 1):
                pl.when(sy + e < NY)(cp.wait_send)

        loop(0, HEADS, body)

    def get_states(n, h, mask):
        swap_copy(n, h).wait_recv()
        mine, other = t_st[n, h].reshape(D, D), r2[n, h].reshape(D, D)
        own_first = jnp.where(low, x_st[n, h].reshape(D, D), y_st[n, h].reshape(D, D))
        first = jnp.where(low, mine, other)
        second = (mine + other) + own_first
        return jnp.where(mask, first, second), jnp.where(mask, second, first)

    def kv_state(h):
        for cp in kv_loads(h):
            cp.wait()
        kv = [mm(k_ref[rows(s), cols(h)], v_ref[rows(s), cols(h)], 0, 0) for s in range(2)]
        put_state(0, h, kv[0], kv[1], first0)

    kv_state(0)
    pl.semaphore_wait(bar, len(peers))
    stage_straight(0)
    tell(y_in, at(ys[0], x, core))
    tell(z2_in, z_at(1))
    tell(z2_in, z_at(-1))

    def next_kv(h):
        kv_state(h)
        core_copy(0, h).start()

    loop(1, HEADS, next_kv)
    loop(1, HEADS, lambda h: stage_x(0, h))
    for cp in loads:
        cp.wait()
    gain = gain_ref[...].astype(F32).reshape(1, HEADS * D)
    for h in range(HEADS):
        gain_rows[h : h + 1] = gain[:, h * D : (h + 1) * D]

    def local_attn(h):
        for s in range(2):
            qt[s, h] = jnp.transpose(q_ref[rows(s), cols(h)])
            up[s, h] = g_ref[rows(s), cols(h)].astype(F32) * gain_rows[pl.ds(h, 1)]
            scores = jnp.where(causal, mm(q_ref[rows(s), cols(h)], k_ref[rows(s), cols(h)], 1, 1), 0.0)
            hi, lo = parts(scores)
            s_hi[s, h] = hi
            s_lo[s, h] = lo
            vv = v_ref[rows(s), cols(h)]
            attn[s, h] = mm(wide(hi, lo), tall(vv, vv), 1, 0)

    pl.semaphore_wait(y_in, 1)
    stage_y_straight(0)
    local_attn(0)

    def next_y(h):
        stage_y(0, h)
        local_attn(h)

    loop(1, HEADS, next_y)
    pl.semaphore_wait(z2_in, 2)
    tell(z4_in, z_at(2))
    tell(z4_in, z_at(2))
    tell(z4_in, z_at(-2))
    sq[...] = jnp.zeros_like(sq)
    cr[...] = jnp.zeros_like(cr)
    loop(0, HEADS, lambda h: stage_back(0, h))
    loop(0, HEADS, lambda h: stage_swap(0, h))

    def full_attn(h):
        prefix = get_states(0, h, first0)
        for s in range(2):
            hi, lo = parts(prefix[s])
            p_hi[s, h] = hi
            p_lo[s, h] = lo
            qq = q_ref[rows(s), cols(h)]
            a = attn[s, h] + mm(wide(qq, qq), tall(hi, lo), 1, 0)
            attn[s, h] = a
            sq[s] += a * a
            cr[s] += up[s, h] * a

    loop(0, HEADS, full_attn)

    zero = jnp.zeros((8 - 4, D), F32)
    zbuf[z] = tall(*[jnp.sum(jnp.transpose(m), axis=0, keepdims=True) for m in (sq[0], sq[1], cr[0], cr[1])], zero)
    pl.semaphore_wait(z4_in, 3)
    start([remote(zbuf.at[z], zbuf.at[z], z_s, z_r, {"head": zz}) for zz in zs])
    seven = zbuf.at[pl.ds(0, NZ - 1)]
    z_all = remote(seven, seven, z_s, z_r, sibling)
    drain_first(0)
    drain_y(0)
    loop(0, HEADS, lambda h: sent([back_all(0, h), swap_copy(0, h)]))
    z_all.wait_recv()
    sums = zbuf[0]
    for i in range(1, NZ):
        sums = sums + zbuf[i]
    features = float(HEADS * D * NZ)
    inverse = lax.rsqrt(sums[0:2] * (1.0 / features) + 1e-6)
    coef = sums[2:4] * (inverse * inverse * inverse) * (1.0 / features)
    for s in range(2):
        inv_b[s] = jnp.transpose(jnp.broadcast_to(inverse[s : s + 1], (D, D)))
        coef_b[s] = jnp.transpose(jnp.broadcast_to(coef[s : s + 1], (D, D)))

    def adjoint(h):
        adj = []
        for s in range(2):
            hi, lo = parts(up[s, h] * inv_b[s] - attn[s, h] * coef_b[s])
            a_hi[s, h] = hi
            a_lo[s, h] = lo
            qq = qt[s, h]
            adj.append(mm(wide(qq, qq), tall(hi, lo), 1, 0))
        put_state(1, h, adj[0], adj[1], last0)

    adjoint(0)
    stage_straight(1)

    def next_adjoint(h):
        adjoint(h)
        core_copy(1, h).start()

    loop(1, HEADS, next_adjoint)

    def local_grads(h):
        for s in range(2):
            ah, al = a_hi[s, h], a_lo[s, h]
            sh, sl = s_hi[s, h], s_lo[s, h]
            ph, pw = p_hi[s, h], p_lo[s, h]
            qq, kk, vv = (r[rows(s), cols(h)] for r in (q_ref, k_ref, v_ref))
            gs = jnp.where(causal, mm(wide(ah, al), wide(vv, vv), 1, 1), 0.0)
            gh, gl = parts(gs)
            gq = mm(wide(gh, gl), tall(kk, kk), 1, 0) + mm(wide(ah, al, ah), wide(ph, ph, pw), 1, 1)
            oq_ref[rows(s), cols(h)] = gq.astype(BF16)
            gk_loc[s, h] = mm(tall(gh, gl), tall(qq, qq), 0, 0)
            gv_loc[s, h] = mm(tall(sh, sl, sh), tall(ah, ah, al), 0, 0)

    def gain_term(h):
        terms = [g_ref[rows(s), cols(h)].astype(F32) * attn[s, h] * inv_b[s] for s in range(2)]
        gcore[core, pl.ds(h, 1)] = jnp.sum(terms[0] + terms[1], axis=0, keepdims=True)

    def gain_send(buf, me, ssem, rsem, devices):
        copies = [remote(buf.at[me], buf.at[me], ssem.at[d], rsem.at[d], device) for d, device in enumerate(devices)]
        start(copies)
        return copies

    def gain_sum(buf, count, copies):
        received(copies)
        total = buf[0]
        for i in range(1, count):
            total = total + buf[i]
        return total

    loop(1, HEADS, lambda h: stage_x(1, h))
    gcore[core] = jnp.zeros((8, D), F32)
    loop(0, HEADS, gain_term)
    gain_1 = gain_send(gcore, core, gc_s, gc_r, [sibling])
    z_all.wait_send()
    stage_y_straight(1)
    local_grads(0)
    gx[x] = gain_sum(gcore, 2, gain_1)
    gain_2 = gain_send(gx, x, gx_s, gx_r, [at(y, v, core) for v in xs])

    def next_grads(h):
        stage_y(1, h)
        local_grads(h)

    loop(1, HEADS, next_grads)
    gy[y] = gain_sum(gx, NX, gain_2)
    gain_3 = gain_send(gy, y, gy_s, gy_r, [at(v, x, core) for v in ys])
    drain_first(1)
    loop(0, HEADS, lambda h: stage_back(1, h))
    gdp[dp] = gain_sum(gy, NY, gain_3)
    gain_4 = gain_send(gdp, dp, gd_s, gd_r, [{"dp": 1 - dp}])
    loop(0, HEADS, lambda h: stage_swap(1, h))
    drain_y(1)
    loop(0, HEADS, lambda h: back_all(1, h).wait_send())
    sent(gain_1 + gain_2 + gain_3 + gain_4)

    def last_grads(h):
        suffix = get_states(1, h, last0)
        for s in range(2):
            hi, lo = parts(suffix[s])
            kk, vv = (r[rows(s), cols(h)] for r in (k_ref, v_ref))
            gk = gk_loc[s, h] + mm(wide(vv, vv), wide(hi, lo), 1, 1)
            gv = gv_loc[s, h] + mm(wide(kk, kk), tall(hi, lo), 1, 0)
            ok_ref[rows(s), cols(h)] = gk.astype(BF16)
            ov_ref[rows(s), cols(h)] = gv.astype(BF16)

    loop(0, HEADS, last_grads)
    gg_ref[...] = gain_sum(gdp, 2, gain_4)
    loop(0, HEADS, lambda h: swap_copy(1, h).wait_send())


def write_kernel(gq, gk, gv, gg, oq, ok, ov, og, line, sem):
    copies = [pltpu.make_async_copy(src, dst, sem.at[i]) for i, (src, dst) in enumerate(((gq, oq), (gk, ok), (gv, ov), (line, og)))]
    for cp in copies[:3]:
        cp.start()
    for h in range(HEADS):
        line[pl.ds(h * D, D)] = gg[h]
    copies[3].start()
    for cp in copies:
        cp.wait()


def shards(queries, keys, values, grad_out, gain, order_flag):
    shape = queries.shape
    tokens, width = shape[1], shape[2]
    flat = [a.reshape(tokens, width) for a in (queries, keys, values, grad_out)]
    gain = pltpu.with_memory_space_constraint(gain, pltpu.HBM)
    state = (2, HEADS, D, D)
    quarters = (2, HEADS, NX, PART, D)
    piece = (HEADS, PART, D)
    dma = pltpu.SemaphoreType.DMA
    scratch = [pltpu.VMEM((tokens, width), BF16)] * 4 + [pltpu.VMEM((width,), BF16), pltpu.VMEM((8, D), F32)]
    scratch += [pltpu.VMEM(quarters, F32)] * 4
    scratch += [
        pltpu.VMEM((2, NX) + piece, F32),
        pltpu.VMEM((2,) + piece, F32),
        pltpu.VMEM((2, NY - 1) + piece, F32),
        pltpu.VMEM((2, NX) + piece, F32),
    ]
    scratch += [pltpu.VMEM(quarters, F32)] * 3
    scratch += [pltpu.VMEM((2, NX, PART, D), F32)]
    scratch += [pltpu.VMEM(state, F32)]
    scratch += [pltpu.VMEM(state, BF16)] * 7
    scratch += [pltpu.VMEM(state, F32)] * 3
    scratch += [pltpu.VMEM((2, D, D), F32)] * 4
    scratch += [pltpu.VMEM((n, 8, D), F32) for n in (NZ, 2, NX, NY, 2)]
    scratch += [pltpu.SemaphoreType.REGULAR] * 3 + [dma((3,)), dma((2, HEADS))]
    for shape_of in ((2, HEADS), (2, HEADS), (2, HEADS, NY - 1), (2, HEADS), (2, HEADS)):
        scratch += [dma(shape_of)] * 2
    scratch += [dma((2,))] * 2 + [dma] * 2
    for count in (1, NX - 1, NY - 1, 1):
        scratch += [dma((count,))] * 2
    hbm = pl.BlockSpec(memory_space=pl.ANY)
    vmem = pl.BlockSpec(memory_space=pltpu.VMEM)
    out = jax.ShapeDtypeStruct((tokens, width), BF16)
    inner = pltpu.VMEM((tokens, width), BF16)
    flat = [pltpu.with_memory_space_constraint(a, pltpu.HBM) for a in flat]
    gq, gk, gv, gg = pl.pallas_call(
        kernel,
        name="layer_backward",
        out_shape=(inner, inner, inner, pltpu.VMEM((8, D), F32)),
        in_specs=[pl.BlockSpec(memory_space=pltpu.SMEM), hbm, hbm, hbm, hbm, hbm],
        out_specs=(vmem, vmem, vmem, vmem),
        scratch_shapes=scratch,
        compiler_params=pltpu.CompilerParams(
            collective_id=0, has_side_effects=True, vmem_limit_bytes=32 * 1024 * 1024
        ),
    )(order_flag, gain, *flat)
    results = [pltpu.with_memory_space_constraint(a, pltpu.VMEM) for a in (gq, gk, gv, gg)]
    gq, gk, gv, gg = pl.pallas_call(
        write_kernel,
        name="write_results",
        out_shape=(out, out, out, jax.ShapeDtypeStruct((width,), F32)),
        in_specs=[vmem, vmem, vmem, vmem],
        out_specs=(hbm, hbm, hbm, hbm),
        scratch_shapes=[pltpu.VMEM((width,), F32), dma((4,))],
        compiler_params=pltpu.CompilerParams(vmem_limit_bytes=32 * 1024 * 1024),
    )(*results)
    return gq.reshape(shape), gk.reshape(shape), gv.reshape(shape), gg


def solution(mesh):
    rows = P("dp", "ctx", "head")
    return jax.shard_map(
        shards,
        mesh=mesh,
        in_specs=(rows, rows, rows, rows, P("head"), P("ctx")),
        out_specs=(rows, rows, rows, P("head")),
        check_vma=False,
    )
```

time: 54.9 us -> 53.7 us (0.978)
  Pallas kernels: 53.4 us -> 52.2 us
    pallas_call x1, Pallas kernels: 52.5 us -> 51.2 us  [shards(): pl.pallas_call(kernel, name='layer_backward', out_shape=(inner, inner, in...]
where the time goes in v5:
time: 53.7 us; the launch traced here: 53.5 us
  Pallas kernels  52.2 us (97%)
  between operations  1.29 us (2%)
    pallas_call x1, Pallas kernels, shards(): pl.pallas_call(kernel, name='layer_backward', out_shape=(inner, inner, in...  51.2 us

profile of v5, /device:TPU:1, one launch (start us, length us, event | category | flops | bytes accessed | tf_op | source)
XLA Modules:
  0.0 53.5 jit_solution(9431507893033281343)
XLA Ops:
  1.3 51.2 %layer_backward.1 = (bf16[256,640]{1,0:T(8,128)(2,1)S(1)}, bf16[256,640]{1,0:T(8,128)(2,1)S(1)}, bf16[256,640]{1,0:T(8,128)(2,1)S(1)}, f32[8,128]{1,0:T(8,128)S(1)}) custom-call(s32[1]{0:T(128)S(6)} %copy.10.flag_ref, bf16[640]{0:T(1024)(128)(2,1)} %gain_hbm.1, bf16[256,640]{1,0:T(8,128)(2,1)} %bitcast.7, bf16[256,640]{1,0:T(8,128)(2,1)} %bitcast.8, ...), custom_call_target="tpu_custom_call" | custom-call | tf_op jit(solution)/shard_map/layer_backward/pallas_call | solution.py:464
  52.5 1.0 %write_results.1 = (bf16[256,640]{1,0:T(8,128)(2,1)}, bf16[256,640]{1,0:T(8,128)(2,1)}, bf16[256,640]{1,0:T(8,128)(2,1)}, f32[640]{0:T(1024)}) custom-call(bf16[256,640]{1,0:T(8,128)(2,1)S(1)} %get-tuple-element.12.gq, bf16[256,640]{1,0:T(8,128)(2,1)S(1)} %get-tuple-element.13.gk, bf16[256,640]{1,0:T(8,128)(2,1)S(1)} %get-tuple-element.14.gv, ...), custom_call_target="tpu_custom_call" | custom-call | tf_op jit(solution)/shard_map/write_results/pallas_call | solution.py:476

commit v6 on v5

--- a/solution.py
+++ b/solution.py
@@ -136,7 +136,7 @@
         for e in range(1, NY):
             yy = jnp.where(core == 0, lax.rem(y + e, NY), lax.rem(y + NY - e, NY))
             out.append(
-                remote(w_st.at[n, h], yr.at[n, e - 1, h], y_s.at[n, h, e - 1], y_r.at[n, h, e - 1], at(yy, x, core))
+                remote(w_st.at[n, h], yr.at[n, e - 1, h], y_s.at[n, h], y_r.at[n, h], at(yy, x, core))
             )
         return out
 
@@ -153,6 +153,10 @@
 
     def straight_all(n):
         return remote(xo.at[n], xo.at[n], xo_s.at[n], xo_r.at[n], sibling)
+
+    def y_all(n, h, count):
+        sums = yr.at[n, pl.ds(0, count), h]
+        return remote(sums, sums, y_s.at[n, h], y_r.at[n, h], sibling)
 
     def back_all(n, h):
         three = t_st.at[n, h, pl.ds(0, NX - 1)]
@@ -200,8 +204,8 @@
             pl.when(sy + e < NY)(copies[e - 1].start)
 
     def stage_back(n, h):
-        for e, cp in enumerate(y_copies(n, h), 1):
-            pl.when(sy >= e)(cp.wait_recv)
+        for count in range(1, NY):
+            pl.when(sy == count)(y_all(n, h, count).wait_recv)
         total = (yr[n, 0, h] + yr[n, 1, h]) + yr[n, 2, h]
         for t in range(NX):
             o_st[n, t, h] = total
@@ -225,8 +229,8 @@
 
     def drain_y(n):
         def body(h):
-            for e, cp in enumerate(y_copies(n, h), 1):
-                pl.when(sy + e < NY)(cp.wait_send)
+            for count in range(1, NY):
+                pl.when(sy + count == NY - 1)(y_all(n, h, count).wait_send)
 
         loop(0, HEADS, body)
 
@@ -363,12 +367,12 @@
         gcore[core, pl.ds(h, 1)] = jnp.sum(terms[0] + terms[1], axis=0, keepdims=True)
 
     def gain_send(buf, me, ssem, rsem, devices):
-        copies = [remote(buf.at[me], buf.at[me], ssem.at[d], rsem.at[d], device) for d, device in enumerate(devices)]
-        start(copies)
-        return copies
+        start([remote(buf.at[me], buf.at[me], ssem, rsem, device) for device in devices])
+        some = buf.at[pl.ds(0, len(devices))]
+        return remote(some, some, ssem, rsem, sibling)
 
     def gain_sum(buf, count, copies):
-        received(copies)
+        copies.wait_recv()
         total = buf[0]
         for i in range(1, count):
             total = total + buf[i]
@@ -398,7 +402,7 @@
     loop(0, HEADS, lambda h: stage_swap(1, h))
     drain_y(1)
     loop(0, HEADS, lambda h: back_all(1, h).wait_send())
-    sent(gain_1 + gain_2 + gain_3 + gain_4)
+    sent([gain_1, gain_2, gain_3, gain_4])
 
     def last_grads(h):
         suffix = get_states(1, h, last0)
@@ -451,11 +455,8 @@
     scratch += [pltpu.VMEM((2, D, D), F32)] * 4
     scratch += [pltpu.VMEM((n, 8, D), F32) for n in (NZ, 2, NX, NY, 2)]
     scratch += [pltpu.SemaphoreType.REGULAR] * 3 + [dma((3,)), dma((2, HEADS))]
-    for shape_of in ((2, HEADS), (2, HEADS), (2, HEADS, NY - 1), (2, HEADS), (2, HEADS)):
-        scratch += [dma(shape_of)] * 2
-    scratch += [dma((2,))] * 2 + [dma] * 2
-    for count in (1, NX - 1, NY - 1, 1):
-        scratch += [dma((count,))] * 2
+    scratch += [dma((2, HEADS))] * 10
+    scratch += [dma((2,))] * 2 + [dma] * 10
     hbm = pl.BlockSpec(memory_space=pl.ANY)
     vmem = pl.BlockSpec(memory_space=pltpu.VMEM)
     out = jax.ShapeDtypeStruct((tokens, width), BF16)

time: 53.7 us -> 53.2 us (level)
  no operation moved by 1% of the time
where the time goes in v6:
time: 53.2 us; the launch traced here: 53.1 us
  Pallas kernels  51.8 us (97%)
  between operations  1.29 us (2%)
    pallas_call x1, Pallas kernels, shards(): pl.pallas_call(kernel, name='layer_backward', out_shape=(inner, inner, in...  50.8 us

profile of v6, /device:TPU:1, one launch (start us, length us, event | category | flops | bytes accessed | tf_op | source)
XLA Modules:
  0.0 53.1 jit_solution(3729980514033630893)
XLA Ops:
  1.3 50.8 %layer_backward.1 = (bf16[256,640]{1,0:T(8,128)(2,1)S(1)}, bf16[256,640]{1,0:T(8,128)(2,1)S(1)}, bf16[256,640]{1,0:T(8,128)(2,1)S(1)}, f32[8,128]{1,0:T(8,128)S(1)}) custom-call(s32[1]{0:T(128)S(6)} %copy.10.flag_ref, bf16[640]{0:T(1024)(128)(2,1)} %gain_hbm.1, bf16[256,640]{1,0:T(8,128)(2,1)} %bitcast.7, bf16[256,640]{1,0:T(8,128)(2,1)} %bitcast.8, ...), custom_call_target="tpu_custom_call" | custom-call | tf_op jit(solution)/shard_map/layer_backward/pallas_call | solution.py:465
  52.1 1.0 %write_results.1 = (bf16[256,640]{1,0:T(8,128)(2,1)}, bf16[256,640]{1,0:T(8,128)(2,1)}, bf16[256,640]{1,0:T(8,128)(2,1)}, f32[640]{0:T(1024)}) custom-call(bf16[256,640]{1,0:T(8,128)(2,1)S(1)} %get-tuple-element.12.gq, bf16[256,640]{1,0:T(8,128)(2,1)S(1)} %get-tuple-element.13.gk, bf16[256,640]{1,0:T(8,128)(2,1)S(1)} %get-tuple-element.14.gv, ...), custom_call_target="tpu_custom_call" | custom-call | tf_op jit(solution)/shard_map/write_results/pallas_call | solution.py:477
